TPU v7x, 128 devices: a whole 4x4x4 slice. The times are simulated.
128 devices in a mesh: tm: 8 (over z, core), space: 16 (over x, y).
Axes of the slice: x: 4, y: 4, z: 4, core: 2. Of those that a mesh axis runs over, the one named last changes fastest.
Arguments:
- increment: float32 [16, 4, 256, 1440], P('tm', None, 'space'), may hold values from -4 to 4
- forcing: float32 [16, 4, 256, 1440], P('tm', None, 'space'), may hold values from -4 to 4
- lat_courant: float32 [4, 256, 1440], P(None, 'space'), may hold values from 0.05 to 0.45
- lon_courant: float32 [4, 256, 1440], P(None, 'space'), may hold values from 0.05 to 0.45
- error_weight: float32 [4, 256, 1440], P(None, 'space'), may hold values from 0.5 to 4
- site_index: int32 [16, 4, 32768], P('tm', None, 'space'), may hold values from 0 to 92159
- site_count: int32 [16, 4, 16], P('tm', None, 'space'), may hold values from 1024 to 2048, as said below
- site_value: float32 [16, 4, 32768], P('tm', None, 'space'), may hold values from -6 to 6
- site_weight: float32 [16, 4, 32768], P('tm', None, 'space'), may hold values from 0.5 to 4
- pair_step: bfloat16 [8, 16, 4, 256, 1440], P(None, 'tm', None, 'space'), may hold values from -24 to 24
- pair_change: bfloat16 [8, 16, 4, 256, 1440], P(None, 'tm', None, 'space'), may hold values from -108 to 108, as said below
Outputs:
- gradient: float32 [16, 4, 256, 1440], P('tm', None, 'space')
- direction: float32 [16, 4, 256, 1440], P('tm', None, 'space')
Inputs may be any that keep to these rules, and one draw needn't show every extreme that they name: `site_count`: in every step and sub-window some tile has all 2048 slots live, and every tile at least half of them. `pair_change`: each entry has the sign of the matching entry of pair_step, so that <y_i, s_i> > 0.
All inputs are finite; a program needn't handle non-finite values.
Results may differ from a plain program's by a relative error of at most 0.0003.
Values sent between devices are 32-bit elements; how exact they have to be, the bound alone decides.
No kernel may reach another device: no remote copies, remote signals or barrier semaphores. Data moves between devices by JAX's collectives and lax.ppermute only.
A program may use at most 128 MiB of HBM per device.

v0:
```python
import jax
import jax.numpy as jnp
from jax import lax
from jax.sharding import PartitionSpec as P

NSTEP = 4


def from_behind(shard, axis, by):
    count = lax.axis_size(axis)
    pairs = [(i, i + by) for i in range(count) if 0 <= i + by < count]
    return lax.ppermute(shard, axis, pairs)


def step_tangent(state, above, lat_courant, lon_courant, forcing):
    left = jnp.roll(state, 1, axis=-1)
    return (
        (1.0 - lat_courant - lon_courant) * state
        + lat_courant * above
        + lon_courant * left
        + forcing
    )


def tangent(state, lat_courant, lon_courant, forcing):
    top = from_behind(state[:, :, -1:, :], "space", 1)
    above = jnp.concatenate([top, state[:, :, :-1, :]], axis=2)
    return step_tangent(state, above, lat_courant, lon_courant, forcing)


def step_adjoint(dual, below, lat_courant, lon_courant):
    right = jnp.roll(lon_courant * dual, -1, axis=-1)
    return (1.0 - lat_courant - lon_courant) * dual + below + right


def adjoint(dual, lat_courant, lon_courant):
    lat_part = lat_courant * dual
    bottom = from_behind(lat_part[:, :, :1, :], "space", -1)
    below = jnp.concatenate([lat_part[:, :, 1:, :], bottom], axis=2)
    return step_adjoint(dual, below, lat_courant, lon_courant)


def inject(weights, cells, total):

    def single(values, where):
        return jnp.zeros((total,), jnp.float32).at[where].add(values)

    return jax.vmap(single)(weights, cells)


def on_device(
    increment,
    forcing,
    lat_courant,
    lon_courant,
    error_weight,
    site_index,
    site_count,
    site_value,
    site_weight,
    pair_step,
    pair_change,
):
    subs, levels, rows, longs = increment.shape
    total = levels * rows * longs
    pairs = pair_step.shape[0]
    slots = site_index.shape[2]
    live = jnp.arange(slots, dtype=jnp.int32)[None, None, :] < site_count
    state = increment
    deps = []
    for step in range(NSTEP):
        state = tangent(state, lat_courant, lon_courant, forcing)
        seen = jnp.take_along_axis(state.reshape(subs, total), site_index[:, step], axis=1)
        deps.append(
            jnp.where(live[:, step], site_weight[:, step] * (site_value[:, step] - seen), 0.0)
        )
    arrived = from_behind(state[-1], "tm", 1)
    previous = jnp.concatenate([arrived[None], state[:-1]], axis=0)
    weighted = error_weight * (increment - previous)
    later = from_behind(weighted[0], "tm", -1)
    dual = jnp.concatenate([weighted[1:], later[None]], axis=0)
    injections = [
        inject(deps[step], site_index[:, step], total).reshape(dual.shape) for step in range(NSTEP)
    ]
    for step in range(NSTEP - 1, -1, -1):
        dual = dual + injections[step]
        dual = adjoint(dual, lat_courant, lon_courant)
    gradient = weighted - dual
    newest = pair_change[pairs - 1].astype(jnp.float32)
    local_stats = [
        jnp.sum(pair_change[i].astype(jnp.float32) * pair_step[i].astype(jnp.float32))
        for i in range(pairs)
    ]
    local_stats.append(jnp.sum(newest * newest))
    stats = lax.psum(jnp.stack(local_stats), ("tm", "space"))
    gamma = stats[pairs - 1] / stats[pairs]
    vector = gradient
    alphas = [None] * pairs
    for i in range(pairs - 1, -1, -1):
        local_dot = jnp.sum(pair_step[i].astype(jnp.float32) * vector)
        alphas[i] = 1.0 / stats[i] * lax.psum(local_dot, ("tm", "space"))
        vector = vector - alphas[i] * pair_change[i].astype(jnp.float32)
    result = gamma * vector
    for i in range(pairs):
        local_dot = jnp.sum(pair_change[i].astype(jnp.float32) * result)
        beta = 1.0 / stats[i] * lax.psum(local_dot, ("tm", "space"))
        result = result + (alphas[i] - beta) * pair_step[i].astype(jnp.float32)
    return (gradient, result)


def solution(mesh):
    return jax.shard_map(
        on_device,
        mesh=mesh,
        in_specs=(
            P("tm", None, "space", None),
            P("tm", None, "space", None),
            P(None, "space", None),
            P(None, "space", None),
            P(None, "space", None),
            P("tm", None, "space"),
            P("tm", None, "space"),
            P("tm", None, "space"),
            P("tm", None, "space"),
            P(None, "tm", None, "space", None),
            P(None, "tm", None, "space", None),
        ),
        out_specs=(P("tm", None, "space", None), P("tm", None, "space", None)),
        check_vma=False,
    )
```

profile of v0, /device:TPU:1, one launch (start us, length us, event | category | flops | bytes accessed | tf_op | source)
XLA Modules:
  0.0 1410.0 jit_solution(13137666080079620641)
XLA Ops:
  1.8 4.0 collective-permute-start
  12.1 3.2 collective-permute-start.1
  17.0 3.7 collective-permute-start.2
  24.3 3.7 collective-permute-start.3
  31.5 7.7 collective-permute-start.4
  39.3 4.6 collective-permute-done.4
  48.2 34.9 %gather_fusion.3 = f32[4096]{0:T(1024)S(1)} fusion(f32[2,92160]{1,0:T(2,128)S(1)} %reshape.207, s32[4096]{0:T(1024)S(1)} %bitcast.316), kind=kCustom, calls=%fused_computation.3.clone | custom fusion | bytes 65536 | tf_op jit(solution)/shard_map/jit(take_along_axis)/gather | solution.py:73
  84.1 34.9 %gather_fusion.2 = f32[4096]{0:T(1024)S(1)} fusion(f32[2,92160]{1,0:T(2,128)S(1)} %reshape.205, s32[4096]{0:T(1024)S(1)} %bitcast.314), kind=kCustom, calls=%fused_computation.2.clone | custom fusion | bytes 65536 | tf_op jit(solution)/shard_map/jit(take_along_axis)/gather | solution.py:73
  121.0 34.9 %gather_fusion.1 = f32[4096]{0:T(1024)S(1)} fusion(f32[2,92160]{1,0:T(2,128)S(1)} %reshape.203, s32[4096]{0:T(1024)S(1)} %bitcast.315), kind=kCustom, calls=%fused_computation.1.clone | custom fusion | bytes 65536 | tf_op jit(solution)/shard_map/jit(take_along_axis)/gather | solution.py:73
  156.8 34.9 %gather_fusion = f32[4096]{0:T(1024)S(1)} fusion(f32[2,92160]{1,0:T(2,128)S(1)} %reshape.201, s32[4096]{0:T(1024)S(1)} %bitcast.313), kind=kCustom, calls=%fused_computation.clone | custom fusion | bytes 65536 | tf_op jit(solution)/shard_map/jit(take_along_axis)/gather | solution.py:73
  191.9 22.1 %scatter_custom_fusion = f32[184320]{0:T(1024)S(1)} fusion(s32[4096]{0:T(1024)S(1)} %bitcast.325, f32[4096]{0:T(1024)S(1)} %bitcast.330, f32[]{:T(128)} %constant.25.clone.1), kind=kCustom, calls=%fused_computation.143 | custom fusion | flops 4096 | bytes 737284
  218.3 22.9 %scatter_custom_fusion.1 = f32[184320]{0:T(1024)} fusion(s32[4096]{0:T(1024)} %bitcast.326, f32[4096]{0:T(1024)S(1)} %bitcast.331, f32[]{:T(128)} %constant.25.clone.1), kind=kCustom, calls=%fused_computation.141 | custom fusion | flops 4096 | bytes 737792
  251.3 22.2 %scatter_custom_fusion.2 = f32[184320]{0:T(1024)S(1)} fusion(s32[4096]{0:T(1024)S(1)} %bitcast.328, f32[4096]{0:T(1024)} %bitcast.332, f32[]{:T(128)} %constant.25.clone.1), kind=kCustom, calls=%fused_computation.139 | custom fusion | flops 4096 | bytes 737792
  281.5 22.1 %scatter_custom_fusion.3 = f32[184320]{0:T(1024)S(1)} fusion(s32[4096]{0:T(1024)S(1)} %bitcast.327, f32[4096]{0:T(1024)S(1)} %bitcast.329, f32[]{:T(128)} %constant.25.clone.1), kind=kCustom, calls=%fused_computation.137 | custom fusion | flops 4096 | bytes 737284
  310.0 5.7 collective-permute-done.9
  318.7 5.6 stack.39
  324.3 78.3 %all-reduce = (f32[9]{0:T(128)S(1)}, f32[]{:T(128)}) all-reduce(f32[9]{0:T(128)S(1)} %stack.39, f32[]{:T(128)} %get-tuple-element.11), channel_id=1, replica_groups=mesh['tm'=8,'space'=16] {'tm','space'}, use_global_device_ids=true, to_apply=%region_13.15 | all-reduce | flops 10 | bytes 80 | tf_op jit(solution)/shard_map/psum | solution.py:95
  406.6 63.7 %psum.121 = f32[]{:T(128)} all-reduce(f32[]{:T(128)} %fusion.2), channel_id=1, replica_groups=mesh['tm'=8,'space'=16] {'tm','space'}, use_global_device_ids=true, to_apply=%region_17.19 | all-reduce | flops 1 | bytes 8 | tf_op jit(solution)/shard_map/psum | solution.py:101
  474.6 62.6 %psum.122 = f32[]{:T(128)} all-reduce(f32[]{:T(128)} %get-tuple-element.33), channel_id=1, replica_groups=mesh['tm'=8,'space'=16] {'tm','space'}, use_global_device_ids=true, to_apply=%region_19.21 | all-reduce | flops 1 | bytes 8 | tf_op jit(solution)/shard_map/psum | solution.py:101
  540.7 64.1 %psum.123 = f32[]{:T(128)} all-reduce(f32[]{:T(128)} %fusion.12), channel_id=1, replica_groups=mesh['tm'=8,'space'=16] {'tm','space'}, use_global_device_ids=true, to_apply=%region_21.23 | all-reduce | flops 1 | bytes 8 | tf_op jit(solution)/shard_map/psum | solution.py:101
  608.2 62.5 %psum.124 = f32[]{:T(128)} all-reduce(f32[]{:T(128)} %fusion.17), channel_id=1, replica_groups=mesh['tm'=8,'space'=16] {'tm','space'}, use_global_device_ids=true, to_apply=%region_23.25 | all-reduce | flops 1 | bytes 8 | tf_op jit(solution)/shard_map/psum | solution.py:101
  675.2 64.1 %psum.125 = f32[]{:T(128)} all-reduce(f32[]{:T(128)} %get-tuple-element.31), channel_id=1, replica_groups=mesh['tm'=8,'space'=16] {'tm','space'}, use_global_device_ids=true, to_apply=%region_25.27 | all-reduce | flops 1 | bytes 8 | tf_op jit(solution)/shard_map/psum | solution.py:101
  743.9 62.6 %psum.126 = f32[]{:T(128)} all-reduce(f32[]{:T(128)} %fusion.27), channel_id=1, replica_groups=mesh['tm'=8,'space'=16] {'tm','space'}, use_global_device_ids=true, to_apply=%region_27.29 | all-reduce | flops 1 | bytes 8 | tf_op jit(solution)/shard_map/psum | solution.py:101
  810.7 64.1 %psum.127 = f32[]{:T(128)} all-reduce(f32[]{:T(128)} %get-tuple-element.29), channel_id=1, replica_groups=mesh['tm'=8,'space'=16] {'tm','space'}, use_global_device_ids=true, to_apply=%region_29.31 | all-reduce | flops 1 | bytes 8 | tf_op jit(solution)/shard_map/psum | solution.py:101
  878.0 62.5 %psum.128 = f32[]{:T(128)} all-reduce(f32[]{:T(128)} %fusion.37), channel_id=1, replica_groups=mesh['tm'=8,'space'=16] {'tm','space'}, use_global_device_ids=true, to_apply=%region_31.33 | all-reduce | flops 1 | bytes 8 | tf_op jit(solution)/shard_map/psum | solution.py:106
  944.1 64.3 %psum.129 = f32[]{:T(128)} all-reduce(f32[]{:T(128)} %get-tuple-element.27), channel_id=1, replica_groups=mesh['tm'=8,'space'=16] {'tm','space'}, use_global_device_ids=true, to_apply=%region_33.35 | all-reduce | flops 1 | bytes 8 | tf_op jit(solution)/shard_map/psum | solution.py:106
  1011.1 62.5 %psum.130 = f32[]{:T(128)} all-reduce(f32[]{:T(128)} %fusion.26), channel_id=1, replica_groups=mesh['tm'=8,'space'=16] {'tm','space'}, use_global_device_ids=true, to_apply=%region_35.37 | all-reduce | flops 1 | bytes 8 | tf_op jit(solution)/shard_map/psum | solution.py:106
  1077.3 64.1 %psum.131 = f32[]{:T(128)} all-reduce(f32[]{:T(128)} %get-tuple-element.25), channel_id=1, replica_groups=mesh['tm'=8,'space'=16] {'tm','space'}, use_global_device_ids=true, to_apply=%region_37.39 | all-reduce | flops 1 | bytes 8 | tf_op jit(solution)/shard_map/psum | solution.py:106
  1144.1 62.5 %psum.132 = f32[]{:T(128)} all-reduce(f32[]{:T(128)} %fusion.16), channel_id=1, replica_groups=mesh['tm'=8,'space'=16] {'tm','space'}, use_global_device_ids=true, to_apply=%region_39.41 | all-reduce | flops 1 | bytes 8 | tf_op jit(solution)/shard_map/psum | solution.py:106
  1210.4 64.1 %psum.133 = f32[]{:T(128)} all-reduce(f32[]{:T(128)} %get-tuple-element.23), channel_id=1, replica_groups=mesh['tm'=8,'space'=16] {'tm','space'}, use_global_device_ids=true, to_apply=%region_41.43 | all-reduce | flops 1 | bytes 8 | tf_op jit(solution)/shard_map/psum | solution.py:106
  1277.1 62.5 %psum.134 = f32[]{:T(128)} all-reduce(f32[]{:T(128)} %fusion.6), channel_id=1, replica_groups=mesh['tm'=8,'space'=16] {'tm','space'}, use_global_device_ids=true, to_apply=%region_43.45 | all-reduce | flops 1 | bytes 8 | tf_op jit(solution)/shard_map/psum | solution.py:106
  1342.5 64.1 %psum.135 = f32[]{:T(128)} all-reduce(f32[]{:T(128)} %fusion.41), channel_id=1, replica_groups=mesh['tm'=8,'space'=16] {'tm','space'}, use_global_device_ids=true, to_apply=%region_45.47 | all-reduce | flops 1 | bytes 8 | tf_op jit(solution)/shard_map/psum | solution.py:106
  (167 shorter events, 96.1 us)
Async XLA Ops:
  0.6 9.7 copy-start.6
  0.6 9.7 copy-start.3
  0.7 9.7 copy-start.2
  1.8 8.5 collective-permute-start
  10.4 5.0 copy-start.28
  10.4 6.1 copy-start.9
  12.1 4.4 collective-permute-start.1
  16.5 4.2 copy-start.27
  17.0 6.3 copy-start.4
  17.0 4.8 collective-permute-start.2
  21.9 6.1 copy-start.26
  24.3 4.8 collective-permute-start.3
  29.1 14.8 %copy-start.22 = (f32[4,16,1440]{2,1,0:T(8,128)S(1)}, f32[4,16,1440]{2,1,0:T(8,128)}, u32[]{:S(2)}) copy-start(f32[4,16,1440]{2,1,0:T(8,128)} %param.17) | copy-start | bytes 1105924
  31.4 12.6 copy-start.10
  31.4 12.5 copy-start.7
  31.5 13.4 copy-start.12
  31.5 12.4 collective-permute-start.4
  44.8 169.6 %collective-permute-start.5 = (f32[4,16,1440]{2,1,0:T(8,128)}, f32[4,16,1440]{2,1,0:T(8,128)}, u32[]{:S(2)}, u32[]{:S(2)}) collective-permute-start(f32[4,16,1440]{2,1,0:T(8,128)} %get-tuple-element.45), channel_id=1, source_target_pairs={{16,0},{32,16},{48,32},{64,48},{80,64},{96,80},{112,96},{17,1},{33... | collective-permute-start | bytes 1105928 | tf_op jit(solution)/shard_map/ppermute | solution.py:12
  48.2 34.9 %copy-start.5 = (f32[2,4,16,1440]{3,2,1,0:T(8,128)S(1)}, f32[2,4,16,1440]{3,2,1,0:T(8,128)}, u32[]{:S(2)}) copy-start(f32[2,4,16,1440]{3,2,1,0:T(8,128)} %copy-done.4) | copy-start | bytes 2211844
  121.0 34.9 %copy-start.11 = (f32[2,4,16,1440]{3,2,1,0:T(8,128)S(1)}, f32[2,4,16,1440]{3,2,1,0:T(8,128)}, u32[]{:S(2)}) copy-start(f32[2,4,16,1440]{3,2,1,0:T(8,128)} %copy-done.10) | copy-start | bytes 2211844
  216.5 28.8 %collective-permute-start.6 = (f32[2,4,1,1440]{3,2,1,0:T(1,128)S(1)}, f32[2,4,1,1440]{3,2,1,0:T(1,128)S(1)}, u32[]{:S(2)}, u32[]{:S(2)}) collective-permute-start(f32[2,4,1,1440]{3,2,1,0:T(1,128)S(1)} %slice.384), channel_id=1, source_target_pairs={{1,0},{2,1},{3,2},{4,3},{5,4},{6,5},{7,6},{8,7},{9,8},{10,9},{11,1... | collective-permute-start | bytes 138248 | tf_op jit(solution)/shard_map/ppermute | solution.py:12
  248.7 27.5 %copy-start.14 = (f32[2,4,16,1440]{3,2,1,0:T(8,128)S(1)}, f32[2,4,16,1440]{3,2,1,0:T(8,128)}, u32[]{:S(2)}) copy-start(f32[2,4,16,1440]{3,2,1,0:T(8,128)} %get-tuple-element.40) | copy-start | bytes 2211844
  249.4 27.1 %collective-permute-start.7 = (f32[2,4,1,1440]{3,2,1,0:T(1,128)}, f32[2,4,1,1440]{3,2,1,0:T(1,128)}, u32[]{:S(2)}, u32[]{:S(2)}) collective-permute-start(f32[2,4,1,1440]{3,2,1,0:T(1,128)} %slice.389), channel_id=1, source_target_pairs={{1,0},{2,1},{3,2},{4,3},{5,4},{6,5},{7,6},{8,7},{9,8},{10,9},{11,1... | collective-permute-start | bytes 138248 | tf_op jit(solution)/shard_map/ppermute | solution.py:12
  279.5 26.7 %copy-start.15 = (f32[2,4,16,1440]{3,2,1,0:T(8,128)S(1)}, f32[2,4,16,1440]{3,2,1,0:T(8,128)}, u32[]{:S(2)}) copy-start(f32[2,4,16,1440]{3,2,1,0:T(8,128)} %get-tuple-element.38) | copy-start | bytes 2211844
  280.2 26.4 %collective-permute-start.8 = (f32[2,4,1,1440]{3,2,1,0:T(1,128)}, f32[2,4,1,1440]{3,2,1,0:T(1,128)}, u32[]{:S(2)}, u32[]{:S(2)}) collective-permute-start(f32[2,4,1,1440]{3,2,1,0:T(1,128)} %slice.394), channel_id=1, source_target_pairs={{1,0},{2,1},{3,2},{4,3},{5,4},{6,5},{7,6},{8,7},{9,8},{10,9},{11,1... | collective-permute-start | bytes 138248 | tf_op jit(solution)/shard_map/ppermute | solution.py:12
  306.6 9.1 copy-start.1
  307.9 7.8 copy-start.8
  307.9 7.8 copy-start.13
  307.9 7.8 copy-start.23
  307.9 7.8 copy-start.25
  308.0 7.7 copy-start
  308.1 7.6 collective-permute-start.9
  (7 other events, 8.4 us)
where the time goes:
time: 1420 us; the launch traced here: 1410 us
  blocking collectives  1030 us (73%)
  local copies, waits for them, and re-layouts  174 us (12%)
  other arithmetic  147 us (10%)
  starting transfers between devices  30 us (2%)
  between operations  18.3 us (1%)
    psum x8, blocking collectives, on_device(): beta = 1.0 / stats[i] * lax.psum(local_dot, ('tm', 'space'))  507 us
    psum x7, blocking collectives, on_device(): alphas[i] = 1.0 / stats[i] * lax.psum(local_dot, ('tm', 'space'))  444 us
    gather x8, local copies, waits for them, and re-layouts, on_device(): jnp.take_along_axis(state.reshape(subs, total), site_index[:, step], axis=1)  140 us
    unnamed x14, other arithmetic  89.9 us
    psum x1, blocking collectives, on_device(): stats = lax.psum(jnp.stack(local_stats), ('tm', 'space'))  78.3 us
    ppermute x10, starting transfers between devices, from_behind(): return lax.ppermute(shard, axis, pairs)  30 us
  transfers between devices with their start and end apart: 10, of which 5 were waited for; matrix products, arithmetic and copies ran while one was open for 18% of the time, Pallas kernels for 0%

commit v1 on v0

v1 whole, which is shorter than its diff:
```python
import functools

import jax
import jax.numpy as jnp
from jax import lax
from jax.experimental import pallas as pl
from jax.experimental.pallas import tpu as pltpu
from jax.sharding import PartitionSpec as P

NSTEP = 4
LANES = 128
F32 = jnp.float32
BF16 = jnp.bfloat16
WHOLE = pl.BlockSpec(memory_space=pltpu.VMEM)
SCALAR = pl.BlockSpec(memory_space=pltpu.SMEM)


def shifted(shard, axis, by):
    count = lax.axis_size(axis)
    pairs = [(i, i + by) for i in range(count) if 0 <= i + by < count]
    return lax.ppermute(shard, axis, pairs)


def west(x):
    return jnp.concatenate([x[:, -1:], x[:, :-1]], axis=1)


def east(x):
    return jnp.concatenate([x[:, 1:], x[:, :1]], axis=1)


def rows_of(x):
    return lax.broadcasted_iota(jnp.int32, x.shape, 0)


def params(mib):
    return pltpu.CompilerParams(vmem_limit_bytes=mib << 20)


def halves(x):
    high = x.astype(BF16)
    return high, (x - high.astype(F32)).astype(BF16)


def edge_kernel(inc_ref, forcing_ref, lat_ref, lon_ref, out_ref):
    levels = lat_ref.shape[0]
    for j in range(out_ref.shape[0]):
        sub, lev = divmod(j, levels)
        x = inc_ref[sub, lev]
        lat, lon, push = lat_ref[lev], lon_ref[lev], forcing_ref[sub, lev]
        rest = 1.0 - lat - lon
        for step in range(NSTEP):
            out_ref[j, step : step + 1, :] = x[7:8, :]
            if step < NSTEP - 1:
                x = rest * x + lat * pltpu.roll(x, 1, 0) + lon * west(x) + push


def pairs_kernel(step_ref, change_ref, out_ref, acc_ref):
    block = pl.program_id(0)
    pairs, _, _, rows, longs = step_ref.shape
    both = 2 * pairs * rows

    @pl.when(block == 0)
    def _():
        acc_ref[...] = jnp.zeros_like(acc_ref)

    for lev in range(step_ref.shape[2]):
        steps = step_ref[:, 0, lev].reshape(pairs * rows, longs)
        changes = change_ref[:, 0, lev].reshape(pairs * rows, longs)
        left = jnp.concatenate([steps, changes], axis=0)
        acc_ref[...] += lax.dot_general(
            left, changes, (((1,), (1,)), ((), ())), preferred_element_type=F32
        )

    @pl.when(block == pl.num_programs(0) - 1)
    def _():
        total = acc_ref[...]
        row = lax.broadcasted_iota(jnp.int32, total.shape, 0)
        col = lax.broadcasted_iota(jnp.int32, total.shape, 1)
        total = jnp.where(row % rows == col % rows, total, 0.0)
        sums = [
            jnp.sum(total[v * rows : (v + 1) * rows], axis=0, keepdims=True)
            for v in range(both // rows)
        ]
        out_ref[...] = jnp.concatenate(sums, axis=0)


def observe_kernel(
    last_ref,
    inc_ref,
    forcing_ref,
    lat_ref,
    lon_ref,
    ew_ref,
    next_ref,
    above_ref,
    index_ref,
    count_ref,
    value_ref,
    weight_ref,
    end_ref,
    edge_ref,
    inject_ref,
    cell_ref,
    lane_ref,
    dep_ref,
    state_ref,
    hot_ref,
    value_row,
    weight_row,
    live_row,
):
    subs, levels, rows, longs = inc_ref.shape
    slots = index_ref.shape[2]
    tiles = -(-longs // LANES)
    half = tiles * levels * 8
    wide = tiles * LANES
    state_ref[:, :, :, longs - longs % LANES :] = jnp.zeros(
        (subs * NSTEP, levels, rows, LANES), F32
    )

    def tangent(j, _):
        sub, lev = j // levels, j % levels
        x = inc_ref[sub, lev]
        lat, lon, push = lat_ref[lev], lon_ref[lev], forcing_ref[sub, lev]
        rest = 1.0 - lat - lon
        top = rows_of(x) == 0
        for step in range(NSTEP):
            above = jnp.where(top, above_ref[j, step : step + 1, :], pltpu.roll(x, 1, 0))
            x = rest * x + lat * above + lon * west(x) + push
            state_ref[sub * NSTEP + step, lev, :, :longs] = x
        end_ref[sub, lev] = x
        return 0

    lax.fori_loop(0, subs * levels, tangent, 0)

    slot = lax.broadcasted_iota(jnp.int32, (1, slots), 1)
    for sub in range(subs):
        index = index_ref[sub]
        row = ((index.astype(F32) + 0.5) * (1.0 / longs)).astype(jnp.int32)
        lon = index - row * longs
        lat = row % rows
        cell = (lat // 8) * half + (lon // LANES) * (levels * 8) + (row // rows) * 8 + lat % 8
        lane = lon % LANES
        value, weight = value_ref[sub], weight_ref[sub]
        for step in range(NSTEP):
            k = sub * NSTEP + step
            cell_ref[k] = cell[step : step + 1]
            lane_ref[k] = lane[step : step + 1]
            value_row[k] = value[step : step + 1]
            weight_row[k] = weight[step : step + 1]
            live_row[k] = (slot < count_ref[sub, step]).astype(F32)

    def one(k, _):
        cell = cell_ref[k].astype(jnp.int16)
        lane = lane_ref[k].astype(jnp.int16)
        blocks = []
        for first in range(0, 2 * tiles, 4):
            part = []
            for at in range(first, first + 4):
                lower, tile = divmod(at, tiles)
                part.append(
                    state_ref[
                        k, :, lower * 8 : lower * 8 + 8, tile * LANES : (tile + 1) * LANES
                    ].reshape(levels * 8, LANES)
                )
            blocks.append(jnp.concatenate(part, axis=0).T)
        table = jnp.concatenate(halves(jnp.concatenate(blocks, axis=1)), axis=0)
        chunk = 256
        seen = []
        place = lax.broadcasted_iota(jnp.int16, (LANES, chunk), 0)
        for first in range(0, slots, chunk):
            part = slice(first, first + chunk)
            hot = jnp.where(
                lax.broadcasted_iota(jnp.int16, (2 * half, chunk), 0) == cell[:, part],
                jnp.ones((), BF16),
                jnp.zeros((), BF16),
            )
            hot_ref[:, part] = hot[:half]
            got = jnp.dot(table, hot, preferred_element_type=F32)
            got = got[:LANES] + got[LANES:]
            mine = lax.broadcasted_iota(jnp.int32, (LANES, chunk), 0) == lane_ref[k][:, part]
            seen.append(jnp.sum(jnp.where(mine, got, 0.0), axis=0, keepdims=True))
        seen = jnp.concatenate(seen, axis=1)
        dep = jnp.where(live_row[k] > 0.0, weight_row[k] * (value_row[k] - seen), 0.0)
        dep_ref[k] = dep
        inject_ref[k] = spread(hot_ref[...], lane, dep, levels, longs)
        return 0

    lax.fori_loop(0, subs * NSTEP, one, 0)

    for sub in range(subs):
        for lev in range(levels):
            j = sub * levels + lev
            later = next_ref[lev, :8] if sub == subs - 1 else inc_ref[sub + 1, lev, :8]
            d = ew_ref[lev, :8] * (later - end_ref[sub, lev, :8])
            if sub == subs - 1:
                d = d * last_ref[0]
            lat, lon = lat_ref[lev, :8], lon_ref[lev, :8]
            rest = 1.0 - lat - lon
            for step in range(NSTEP - 1, -1, -1):
                d = d + inject_ref[sub * NSTEP + step, lev]
                part = lat * d
                edge_ref[j, step : step + 1, :] = part[:1, :]
                if step:
                    d = rest * d + pltpu.roll(part, 7, 0) + east(lon * d)


def spread(hot, lane, dep, levels, longs):
    slots = dep.shape[1]
    high, low = halves(dep)
    mine = lax.broadcasted_iota(jnp.int16, (LANES, slots), 0) == lane
    zero = jnp.zeros((), BF16)
    values = jnp.concatenate([jnp.where(mine, high, zero), jnp.where(mine, low, zero)], axis=0)
    out = lax.dot_general(hot, values, (((1,), (1,)), ((), ())), preferred_element_type=F32)
    out = out[:, :LANES] + out[:, LANES:]
    band = levels * 8
    tiles = out.shape[0] // band
    parts = [out[t * band : (t + 1) * band] for t in range(tiles)]
    return jnp.concatenate(parts, axis=1)[:, :longs].reshape(levels, 8, longs)


def lower_kernel(cell_ref, lane_ref, dep_ref, inject_ref):
    count, levels, _, longs = inject_ref.shape
    slots = dep_ref.shape[2]
    half = -(-longs // LANES) * levels * 8

    def one(k, _):
        cell = (cell_ref[k] - half).astype(jnp.int16)
        hot = jnp.where(
            lax.broadcasted_iota(jnp.int16, (half, slots), 0) == cell,
            jnp.ones((), BF16),
            jnp.zeros((), BF16),
        )
        inject_ref[k] = spread(hot, lane_ref[k].astype(jnp.int16), dep_ref[k], levels, longs)
        return 0

    lax.fori_loop(0, count, one, 0)


def gradient_kernel(
    last_ref,
    inc_ref,
    lat_ref,
    lon_ref,
    ew_ref,
    next_ref,
    end_ref,
    previous_ref,
    upper_ref,
    lower_ref,
    below_ref,
    gram_ref,
    step_ref,
    change_ref,
    grad_ref,
    stats_ref,
    step_buf,
    change_buf,
    dots_ref,
    sems,
):
    subs, levels, rows, longs = inc_ref.shape
    pairs = step_ref.shape[0]
    count = subs * levels

    def copies(j):
        sub, lev = j // levels, j % levels
        return (
            pltpu.make_async_copy(step_ref.at[:, sub, lev], step_buf.at[j], sems.at[0, j]),
            pltpu.make_async_copy(change_ref.at[:, sub, lev], change_buf.at[j], sems.at[1, j]),
        )

    for j in range(count):
        for copy in copies(j):
            copy.start()
    dots_ref[...] = jnp.zeros_like(dots_ref)

    def one(j, _):
        sub, lev = j // levels, j % levels
        ew = ew_ref[lev]
        final = sub == subs - 1
        later = jnp.where(final, next_ref[lev], inc_ref[jnp.minimum(sub + 1, subs - 1), lev])
        d = ew * (later - end_ref[sub, lev])
        d = d * jnp.where(final, last_ref[0], 1.0)
        lat, lon = lat_ref[lev], lon_ref[lev]
        rest = 1.0 - lat - lon
        bottom = rows_of(d) == rows - 1
        for step in range(NSTEP - 1, -1, -1):
            k = sub * NSTEP + step
            d = d + jnp.concatenate([upper_ref[k, lev], lower_ref[k, lev]], axis=0)
            part = lat * d
            below = jnp.where(
                bottom, below_ref[j, step : step + 1, :], pltpu.roll(part, rows - 1, 0)
            )
            d = rest * d + below + east(lon * d)
        earlier = jnp.where(sub == 0, previous_ref[lev], end_ref[jnp.maximum(sub - 1, 0), lev])
        g = ew * (inc_ref[sub, lev] - earlier) - d
        grad_ref[sub, lev] = g
        for copy in copies(j):
            copy.wait()
        for i in range(pairs):
            for which, buf in enumerate((step_buf, change_buf)):
                dots_ref[which * pairs + i] += fold(g * buf[j, i].astype(F32))
        return 0

    lax.fori_loop(0, count, one, 0)
    sums = [jnp.sum(dots_ref[v], axis=0, keepdims=True) for v in range(2 * pairs)]
    sums = jnp.concatenate(sums, axis=0)
    dots = jnp.sum(sums, axis=1, keepdims=True)
    raw = gram_ref[...]
    row = lax.broadcasted_iota(jnp.int32, raw.shape, 0)
    col = lax.broadcasted_iota(jnp.int32, raw.shape, 1)
    group = col // rows
    here = col % rows == row
    out = jnp.zeros((1, raw.shape[1]), F32)
    for c in range(pairs):
        part = jnp.sum(jnp.where(group == c, raw, 0.0), axis=1, keepdims=True)
        out += jnp.sum(jnp.where(here & (group == c), part, 0.0), axis=0, keepdims=True)
    stats_ref[0:1, :] = out
    stats_ref[1:2, :] = jnp.sum(jnp.where(here, dots, 0.0), axis=0, keepdims=True)


def fold(x):
    longs = x.shape[1]
    whole = longs - longs % LANES
    x = x[:8] + x[8:]
    out = x[:, :LANES]
    for first in range(LANES, whole, LANES):
        out = out + x[:, first : first + LANES]
    if whole < longs:
        tail = jnp.concatenate(
            [x[:, whole:], jnp.zeros((8, LANES - (longs - whole)), F32)], axis=1
        )
        out = out + tail
    return out


def direction_kernel(stats_ref, grad_ref, step_ref, change_ref, out_ref, coef_ref):
    pairs = step_ref.shape[0]
    both = 2 * pairs

    @pl.when(pl.program_id(0) == 0)
    def _():
        gram = jnp.sum(stats_ref[:, 0, :], axis=0, keepdims=True)
        dots = jnp.sum(stats_ref[:, 1, :], axis=0, keepdims=True)
        shape = (both, LANES)
        row = lax.broadcasted_iota(jnp.int32, shape, 0)
        col = lax.broadcasted_iota(jnp.int32, shape, 1)
        group, inner = col // both, col % both
        gram = jnp.broadcast_to(gram, shape)
        dots = jnp.broadcast_to(dots, shape)

        def column(mask, x):
            return jnp.sum(jnp.where(mask, x, 0.0), axis=1, keepdims=True)

        dots = column((inner == row) & (group == 0), dots)
        by_change = [column((inner == row) & (group == c), gram) for c in range(pairs)]
        by_step = [column((group == row) & (inner == i), gram)[:pairs] for i in range(pairs)]
        diagonal = column((group == row) & (inner == row), gram)[:pairs]
        rho = 1.0 / diagonal
        with_step, with_change = dots[:pairs], dots[pairs:]
        alphas = [None] * pairs
        for i in range(pairs - 1, -1, -1):
            alphas[i] = rho[i : i + 1] * with_step[i : i + 1]
            with_step = with_step - alphas[i] * by_change[i][:pairs]
            with_change = with_change - alphas[i] * by_change[i][pairs:]
        gamma = diagonal[pairs - 1 : pairs] / by_change[pairs - 1][both - 1 : both]
        with_change = gamma * with_change
        coef_ref[both] = jnp.broadcast_to(gamma, (8, LANES))
        for i in range(pairs):
            beta = rho[i : i + 1] * with_change[i : i + 1]
            rise = alphas[i] - beta
            with_change = with_change + rise * by_step[i]
            coef_ref[i] = jnp.broadcast_to(rise, (8, LANES))
            coef_ref[pairs + i] = jnp.broadcast_to(-gamma * alphas[i], (8, LANES))

    gamma = coef_ref[both][:1, :1]
    for lev in range(step_ref.shape[2]):
        total = gamma * grad_ref[0, lev]
        for i in range(pairs):
            total += coef_ref[i][:1, :1] * step_ref[i, 0, lev].astype(F32)
            total += coef_ref[pairs + i][:1, :1] * change_ref[i, 0, lev].astype(F32)
        out_ref[0, lev] = total


def on_device(
    increment,
    forcing,
    lat_courant,
    lon_courant,
    error_weight,
    site_index,
    site_count,
    site_value,
    site_weight,
    pair_step,
    pair_change,
):
    subs, levels, rows, longs = increment.shape
    pairs = pair_step.shape[0]
    slots = site_index.shape[2]
    count = subs * levels
    tiles = -(-longs // LANES)
    half = tiles * levels * 8
    devices = lax.axis_size("tm") * lax.axis_size("space")
    last = jnp.where(lax.axis_index("tm") == lax.axis_size("tm") - 1, 0.0, 1.0)
    last = last.astype(F32).reshape(1)

    following = shifted(increment[0], "tm", -1)
    edge = pl.pallas_call(
        edge_kernel,
        grid=(1,),
        in_specs=[
            pl.BlockSpec((subs, levels, 8, longs), lambda i: (0, 0, 1, 0)),
            pl.BlockSpec((subs, levels, 8, longs), lambda i: (0, 0, 1, 0)),
            pl.BlockSpec((levels, 8, longs), lambda i: (0, 1, 0)),
            pl.BlockSpec((levels, 8, longs), lambda i: (0, 1, 0)),
        ],
        out_specs=pl.BlockSpec((count, NSTEP, longs), lambda i: (0, 0, 0)),
        out_shape=jax.ShapeDtypeStruct((count, NSTEP, longs), F32),
        compiler_params=params(16),
        name="edge",
    )(increment, forcing, lat_courant, lon_courant)
    above = shifted(edge, "space", 1)

    some = 2
    pair_spec = pl.BlockSpec(
        (pairs, 1, some, rows, longs), lambda b: (0, b // (levels // some), b % (levels // some), 0, 0)
    )
    blocks = count // some
    gram = pl.pallas_call(
        pairs_kernel,
        grid=(blocks,),
        in_specs=[pair_spec, pair_spec],
        out_specs=pl.BlockSpec((2 * pairs, pairs * rows), lambda b: (0, 0)),
        out_shape=jax.ShapeDtypeStruct((2 * pairs, pairs * rows), F32),
        scratch_shapes=[pltpu.VMEM((2 * pairs * rows, pairs * rows), F32)],
        compiler_params=params(16),
        cost_estimate=pl.CostEstimate(
            flops=2 * 256 * 128 * 184320, bytes_accessed=5898240, transcendentals=0
        ),
        name="pairs",
    )(pair_step, pair_change)

    row_shape = (subs * NSTEP, 1, slots)
    end, edge, upper, cell, lane, dep = pl.pallas_call(
        observe_kernel,
        in_specs=[SCALAR] + [WHOLE] * 8 + [SCALAR] + [WHOLE] * 2,
        out_specs=[WHOLE] * 6,
        out_shape=[
            jax.ShapeDtypeStruct(increment.shape, F32),
            jax.ShapeDtypeStruct((count, NSTEP, longs), F32),
            jax.ShapeDtypeStruct((subs * NSTEP, levels, 8, longs), F32),
            jax.ShapeDtypeStruct(row_shape, jnp.int32),
            jax.ShapeDtypeStruct(row_shape, jnp.int32),
            jax.ShapeDtypeStruct(row_shape, F32),
        ],
        scratch_shapes=[
            pltpu.VMEM((subs * NSTEP, levels, rows, tiles * LANES), F32),
            pltpu.VMEM((half, slots), BF16),
            pltpu.VMEM(row_shape, F32),
            pltpu.VMEM(row_shape, F32),
            pltpu.VMEM(row_shape, F32),
        ],
        compiler_params=params(32),
        name="observe",
    )(
        last,
        increment,
        forcing,
        lat_courant,
        lon_courant,
        error_weight,
        following,
        above,
        site_index,
        site_count.reshape(subs, NSTEP),
        site_value,
        site_weight,
    )
    below = shifted(edge, "space", -1)
    previous = shifted(end[-1], "tm", 1)

    lower = pl.pallas_call(
        lower_kernel,
        in_specs=[WHOLE] * 3,
        out_specs=WHOLE,
        out_shape=jax.ShapeDtypeStruct((subs * NSTEP, levels, 8, longs), F32),
        compiler_params=params(24),
        cost_estimate=pl.CostEstimate(
            flops=2 * 8 * 384 * 2048 * 256, bytes_accessed=2000000, transcendentals=0
        ),
        name="lower",
    )(cell, lane, dep)

    gradient, stats = pl.pallas_call(
        gradient_kernel,
        in_specs=[SCALAR] + [WHOLE] * 11 + [pl.BlockSpec(memory_space=pl.ANY)] * 2,
        out_specs=[WHOLE, WHOLE],
        out_shape=[
            jax.ShapeDtypeStruct(increment.shape, F32),
            jax.ShapeDtypeStruct((2, LANES), F32),
        ],
        scratch_shapes=[
            pltpu.VMEM((count, pairs, rows, longs), BF16),
            pltpu.VMEM((count, pairs, rows, longs), BF16),
            pltpu.VMEM((2 * pairs, 8, LANES), F32),
            pltpu.SemaphoreType.DMA((2, count)),
        ],
        compiler_params=params(32),
        name="gradient",
    )(
        last,
        increment,
        lat_courant,
        lon_courant,
        error_weight,
        following,
        end,
        previous,
        upper,
        lower,
        below,
        gram,
        pair_step,
        pair_change,
    )

    spread_out = jnp.broadcast_to(stats[None], (devices,) + stats.shape)
    stats = lax.all_to_all(spread_out, ("tm", "space"), 0, 0)

    field_spec = pl.BlockSpec(
        (1, some, rows, longs), lambda b: (b // (levels // some), b % (levels // some), 0, 0)
    )
    direction = pl.pallas_call(
        direction_kernel,
        grid=(blocks,),
        in_specs=[
            pl.BlockSpec(stats.shape, lambda b: (0, 0, 0)),
            field_spec,
            pair_spec,
            pair_spec,
        ],
        out_specs=field_spec,
        out_shape=jax.ShapeDtypeStruct(increment.shape, F32),
        scratch_shapes=[pltpu.VMEM((2 * pairs + 1, 8, LANES), F32)],
        compiler_params=params(16),
        name="direction",
    )(stats, gradient, pair_step, pair_change)
    return (gradient, direction)


def solution(mesh):
    return jax.shard_map(
        on_device,
        mesh=mesh,
        in_specs=(
            P("tm", None, "space", None),
            P("tm", None, "space", None),
            P(None, "space", None),
            P(None, "space", None),
            P(None, "space", None),
            P("tm", None, "space"),
            P("tm", None, "space"),
            P("tm", None, "space"),
            P("tm", None, "space"),
            P(None, "tm", None, "space", None),
            P(None, "tm", None, "space", None),
        ),
        out_specs=(P("tm", None, "space", None), P("tm", None, "space", None)),
        check_vma=False,
    )
```

time: 1420 us -> 94.7 us (0.07)
  blocking collectives: 1030 us -> 22.4 us
  local copies, waits for them, and re-layouts: 174 us -> 14.1 us
  other arithmetic: 147 us -> 0 us
  Pallas kernels: 0 us -> 38.1 us
  between operations: 18.3 us -> 0.78 us
  starting transfers between devices: 30 us -> 12.8 us
    psum x16 -> x0, blocking collectives: 1030 us -> none  [the longest x8 507 us: on_device(): beta = 1.0 / stats[i] * lax.psum(local_dot, ('tm', 'space'))]
    gather x8 -> x0, local copies, waits for them, and re-layouts: 140 us -> none  [on_device(): jnp.take_along_axis(state.reshape(subs, total), site_index[:, step], axis=1)]
    unnamed x14 -> x0, other arithmetic: 89.9 us -> none
    reduce_sum x16 -> x0, other arithmetic: 40 us -> none  [the longest x8 19.6 us: on_device(): local_dot = jnp.sum(pair_change[i].astype(jnp.float32) * result)]
    pallas_call x0 -> x6, Pallas kernels: none -> 38.1 us  [the longest x1 18.8 us: on_device(): pl.pallas_call(observe_kernel, in_specs=[SCALAR] + [WHOLE] * 8 + [SCALAR]...]
    all_to_all x0 -> x1, blocking collectives: none -> 22.4 us  [on_device(): stats = lax.all_to_all(spread_out, ('tm', 'space'), 0, 0)]
    ppermute x10 -> x4, starting transfers between devices: 30 us -> 12.8 us  [shifted(): return lax.ppermute(shard, axis, pairs)]
    slice x28 -> x0, local copies, waits for them, and re-layouts: 14.5 us -> none  [the longest x4 3.94 us: adjoint(): below = jnp.concatenate([lat_part[:, :, 1:, :], bottom], axis=2)]
  transfers between devices with their start and end apart: 10 -> 4, of which waited for: 5 -> 2; matrix products, arithmetic and copies ran while one was open for 18% -> 0% of each run, Pallas kernels for 0% -> 10%
where the time goes in v1:
time: 94.7 us; the launch traced here: 93.9 us
  Pallas kernels  38.1 us (40%)
  blocking collectives  22.4 us (24%)
  local copies, waits for them, and re-layouts  14.1 us (15%)
  starting transfers between devices  12.8 us (14%)
  waiting for transfers between devices  5.71 us (6%)
    all_to_all x1, blocking collectives, on_device(): stats = lax.all_to_all(spread_out, ('tm', 'space'), 0, 0)  22.4 us
    pallas_call x1, Pallas kernels, on_device(): pl.pallas_call(observe_kernel, in_specs=[SCALAR] + [WHOLE] * 8 + [SCALAR]...  18.8 us
    ppermute x4, starting transfers between devices, shifted(): return lax.ppermute(shard, axis, pairs)  12.8 us
    unnamed x36, local copies, waits for them, and re-layouts  12.2 us
    pallas_call x1, Pallas kernels, on_device(): pl.pallas_call(gradient_kernel, in_specs=[SCALAR] + [WHOLE] * 11 + [pl.Bl...  6.85 us
    ppermute x4, waiting for transfers between devices, shifted(): return lax.ppermute(shard, axis, pairs)  5.71 us
    pallas_call x1, Pallas kernels, on_device(): pl.pallas_call(lower_kernel, in_specs=[WHOLE] * 3, out_specs=WHOLE, out_s...  4.94 us
    pallas_call x1, Pallas kernels, on_device(): pl.pallas_call(direction_kernel, grid=(blocks,), in_specs=[pl.BlockSpec(s...  3.16 us
  transfers between devices with their start and end apart: 4, of which 2 were waited for; matrix products, arithmetic and copies ran while one was open for 0% of the time, Pallas kernels for 10%

profile of v1, /device:TPU:1, one launch (start us, length us, event | category | flops | bytes accessed | tf_op | source)
XLA Modules:
  0.0 93.9 jit_solution(6078608425190643280)
XLA Ops:
  0.6 0.0 copy-start.5
  0.7 1.8 %slice_bitcast_fusion.1 = f32[4,16,1440]{2,1,0:T(8,128)} fusion(f32[2,4,16,1440]{3,2,1,0:T(8,128)} %inc_ref.5), kind=kLoop, calls=%fused_computation.1 | loop fusion | bytes 737280 | tf_op jit(solution)/shard_map/squeeze | solution.py:410
  2.5 3.6 %collective-permute-start = (f32[4,16,1440]{2,1,0:T(8,128)}, f32[4,16,1440]{2,1,0:T(8,128)}, u32[]{:S(2)}, u32[]{:S(2)}) collective-permute-start(f32[4,16,1440]{2,1,0:T(8,128)} %slice_bitcast_fusion.1), channel_id=1, source_target_pairs={{16,0},{32,16},{48,32},{64,48},{80,64},{96,80},{112,96},{17,1},{33... | collective-permute-start | bytes 1105928 | tf_op jit(solution)/shard_map/ppermute | solution.py:21
  6.1 0.0 copy-start.2
  6.1 1.1 %copy-done.2 = f32[2,4,16,1440]{3,2,1,0:T(8,128)S(1)} copy-done((f32[2,4,16,1440]{3,2,1,0:T(8,128)S(1)}, f32[2,4,16,1440]{3,2,1,0:T(8,128)}, u32[]{:S(2)}) %copy-start.2) | copy-done | bytes 737304
  7.2 1.0 %copy-done.4 = f32[4,16,1440]{2,1,0:T(8,128)S(1)} copy-done((f32[4,16,1440]{2,1,0:T(8,128)S(1)}, f32[4,16,1440]{2,1,0:T(8,128)}, u32[]{:S(2)}) %copy-start.4) | copy-done | bytes 368664
  8.2 1.0 %copy-done.6 = f32[4,16,1440]{2,1,0:T(8,128)S(1)} copy-done((f32[4,16,1440]{2,1,0:T(8,128)S(1)}, f32[4,16,1440]{2,1,0:T(8,128)}, u32[]{:S(2)}) %copy-start.6) | copy-done | bytes 368664
  9.2 1.1 %copy-done.9 = f32[2,4,16,1440]{3,2,1,0:T(8,128)S(1)} copy-done((f32[2,4,16,1440]{3,2,1,0:T(8,128)S(1)}, f32[2,4,16,1440]{3,2,1,0:T(8,128)}, u32[]{:S(2)}) %copy-start.9) | copy-done | bytes 737304
  10.3 1.5 %edge.1 = f32[8,4,1440]{2,1,0:T(4,128)} custom-call(f32[2,4,16,1440]{3,2,1,0:T(8,128)S(1)} %copy-done.2, f32[2,4,16,1440]{3,2,1,0:T(8,128)S(1)} %copy-done.9, f32[4,16,1440]{2,1,0:T(8,128)S(1)} %copy-done.4, f32[4,16,1440]{2,1,0:T(8,128)S(1)} %copy-done.6), custom_call_target="tpu_custom_call" | custom-call | tf_op jit(solution)/shard_map/edge/pallas_call | solution.py:411
  11.8 4.0 %collective-permute-start.1 = (f32[8,4,1440]{2,1,0:T(4,128)}, f32[8,4,1440]{2,1,0:T(4,128)}, u32[]{:S(2)}, u32[]{:S(2)}) collective-permute-start(f32[8,4,1440]{2,1,0:T(4,128)} %edge.1), channel_id=1, source_target_pairs={{0,1},{1,2},{2,3},{3,4},{4,5},{5,6},{6,7},{7,8},{8,9},{9,10},{10,1... | collective-permute-start | bytes 552968 | tf_op jit(solution)/shard_map/ppermute | solution.py:21
  15.8 4.2 %collective-permute-done.1.above_ref = f32[8,4,1440]{2,1,0:T(4,128)} collective-permute-done((f32[8,4,1440]{2,1,0:T(4,128)}, f32[8,4,1440]{2,1,0:T(4,128)}, u32[]{:S(2)}, u32[]{:S(2)}) %collective-permute-start.1) | collective-permute-done | bytes 184352 | tf_op jit(solution)/shard_map/ppermute | solution.py:21
  20.0 0.0 collective-permute-done.next_ref
  20.0 1.1 %copy-done.3 = f32[2,4,16,1440]{3,2,1,0:T(8,128)S(1)} copy-done((f32[2,4,16,1440]{3,2,1,0:T(8,128)S(1)}, f32[2,4,16,1440]{3,2,1,0:T(8,128)}, u32[]{:S(2)}) %copy-start.3) | copy-done | bytes 737304
  21.1 1.0 %copy-done.7 = f32[4,16,1440]{2,1,0:T(8,128)S(1)} copy-done((f32[4,16,1440]{2,1,0:T(8,128)S(1)}, f32[4,16,1440]{2,1,0:T(8,128)}, u32[]{:S(2)}) %copy-start.7) | copy-done | bytes 368664
  22.1 1.1 %copy-done.10 = f32[2,4,16,1440]{3,2,1,0:T(8,128)S(1)} copy-done((f32[2,4,16,1440]{3,2,1,0:T(8,128)S(1)}, f32[2,4,16,1440]{3,2,1,0:T(8,128)}, u32[]{:S(2)}) %copy-start.10) | copy-done | bytes 737304
  23.2 1.0 %copy-done.11 = f32[4,16,1440]{2,1,0:T(8,128)S(1)} copy-done((f32[4,16,1440]{2,1,0:T(8,128)S(1)}, f32[4,16,1440]{2,1,0:T(8,128)}, u32[]{:S(2)}) %copy-start.11) | copy-done | bytes 368664
  24.2 0.8 copy-done.14
  25.1 0.8 copy-done.15
  25.9 0.8 copy-done.16
  26.8 18.8 %observe.1 = (f32[2,4,16,1440]{3,2,1,0:T(8,128)S(1)}, f32[8,4,1440]{2,1,0:T(4,128)S(1)}, f32[8,4,8,1440]{3,2,1,0:T(8,128)S(1)}, s32[8,1,2048]{2,1,0:T(1,128)S(1)...) custom-call(f32[1]{0:T(128)} %bitcast.last_ref, f32[2,4,16,1440]{3,2,1,0:T(8,128)S(1)} %copy-done.3, ...), custom_call_target="tpu_custom_call" | custom-call | tf_op jit(solution)/shard_map/observe/pallas_call | solution.py:447
  45.6 4.0 %collective-permute-start.2 = (f32[4,16,1440]{2,1,0:T(8,128)S(1)}, f32[4,16,1440]{2,1,0:T(8,128)S(1)}, u32[]{:S(2)}, u32[]{:S(2)}) collective-permute-start(f32[4,16,1440]{2,1,0:T(8,128)S(1)} %slice_bitcast_fusion), channel_id=1, source_target_pairs={{0,16},{16,32},{32,48},{48,64},{64,80},{80,96},{96,112},{1,17},{17... | collective-permute-start | bytes 1105928 | tf_op jit(solution)/shard_map/ppermute | solution.py:21
  49.6 2.9 %pairs.1.gram_ref = f32[16,128]{1,0:T(8,128)S(1)} custom-call(bf16[8,2,4,16,1440]{4,3,2,1,0:T(8,128)(2,1)S(1)} %copy-done, bf16[8,2,4,16,1440]{4,3,2,1,0:T(8,128)(2,1)S(1)} %copy-done.1), custom_call_target="tpu_custom_call" | custom-call | flops 12079595520 | bytes 5898240 | tf_op jit(solution)/shard_map/pairs/pallas_call | solution.py:432
  52.5 1.3 %collective-permute-start.3 = (f32[8,4,1440]{2,1,0:T(4,128)S(1)}, f32[8,4,1440]{2,1,0:T(4,128)S(1)}, u32[]{:S(2)}, u32[]{:S(2)}) collective-permute-start(f32[8,4,1440]{2,1,0:T(4,128)S(1)} %get-tuple-element.15), channel_id=1, source_target_pairs={{1,0},{2,1},{3,2},{4,3},{5,4},{6,5},{7,6},{8,7},{9,8},{10,9},{11,1... | collective-permute-start | bytes 552968 | tf_op jit(solution)/shard_map/ppermute | solution.py:21
  53.8 0.0 copy-start.8
  53.8 0.0 copy-start.12
  53.8 4.9 %lower.1.lower_ref = f32[8,4,8,1440]{3,2,1,0:T(8,128)S(1)} custom-call(s32[8,1,2048]{2,1,0:T(1,128)S(1)} %get-tuple-element.12.cell_ref, s32[8,1,2048]{2,1,0:T(1,128)S(1)} %get-tuple-element.13.lane_ref, f32[8,1,2048]{2,1,0:T(1,128)S(1)} %get-tuple-element.14.dep_ref), custom_call_target="tpu_custom_call" | custom-call | flops 3221225472 | bytes 2000000 | tf_op jit(solution)/shard_map/lower/pallas_call | solution.py:485
  58.8 1.5 %collective-permute-done.3.below_ref = f32[8,4,1440]{2,1,0:T(4,128)S(1)} collective-permute-done((f32[8,4,1440]{2,1,0:T(4,128)S(1)}, f32[8,4,1440]{2,1,0:T(4,128)S(1)}, u32[]{:S(2)}, u32[]{:S(2)}) %collective-permute-start.3) | collective-permute-done | bytes 184352 | tf_op jit(solution)/shard_map/ppermute | solution.py:21
  60.3 0.0 collective-permute-done.2.previous_ref
  60.3 6.9 %gradient.1 = (f32[2,4,16,1440]{3,2,1,0:T(8,128)}, f32[2,128]{1,0:T(2,128)S(1)}) custom-call(f32[1]{0:T(128)} %bitcast.last_ref, f32[2,4,16,1440]{3,2,1,0:T(8,128)S(1)} %copy-done.3, f32[4,16,1440]{2,1,0:T(8,128)S(1)} %copy-done.5, f32[4,16,1440]{2,1,0:T(8,128)S(1)} %copy-done.8, f32[4,16,1440]{2,1,0:T(8,128)S(1)} %copy-done.12, ...), custom_call_target="tpu_custom_call" | custom-call | tf_op jit(solution)/shard_map/gradient/pallas_call | solution.py:497
  67.2 22.4 %all_to_all.5.stats_ref = f32[128,2,128]{2,1,0:T(2,128)S(1)} all-to-all(f32[128,2,128]{2,1,0:T(2,128)S(1)} %broadcast_in_dim.2), channel_id=1, replica_groups=mesh['tm'=8,'space'=16] {'tm','space'}, dimensions={0} | all-to-all | bytes 262144 | tf_op jit(solution)/shard_map/all_to_all | solution.py:531
  89.7 1.1 %copy-done.13 = f32[2,4,16,1440]{3,2,1,0:T(8,128)S(1)} copy-done((f32[2,4,16,1440]{3,2,1,0:T(8,128)S(1)}, f32[2,4,16,1440]{3,2,1,0:T(8,128)}, u32[]{:S(2)}) %copy-start.13) | copy-done | bytes 737304
  90.8 3.2 %direction.1 = f32[2,4,16,1440]{3,2,1,0:T(8,128)} custom-call(f32[128,2,128]{2,1,0:T(2,128)S(1)} %all_to_all.5.stats_ref, f32[2,4,16,1440]{3,2,1,0:T(8,128)S(1)} %copy-done.13, bf16[8,2,4,16,1440]{4,3,2,1,0:T(8,128)(2,1)S(1)} %copy-done, bf16[8,2,4,16,1440]{4,3,2,1,0:T(8,128)(2,1)S(1)} %copy-done.1), custom_call_target="tpu_custom_call" | custom-call | tf_op jit(solution)/shard_map/direction/pallas_call | solution.py:536
  (22 shorter events, 0.1 us)
Async XLA Ops:
  0.6 19.3 %copy-start.5 = (f32[4,16,1440]{2,1,0:T(8,128)S(1)}, f32[4,16,1440]{2,1,0:T(8,128)}, u32[]{:S(2)}) copy-start(f32[4,16,1440]{2,1,0:T(8,128)} %lat_ref.5) | copy-start | bytes 1105924
  0.6 19.3 %copy-start.17 = (s32[2,4,1]{1,2,0:T(1,128)S(1)}, s32[2,4,1]{1,2,0:T(1,128)}, u32[]{:S(2)}) copy-start(s32[2,4,1]{1,2,0:T(1,128)} %param.17) | copy-start | bytes 100
  2.5 47.1 %copy-start = (bf16[8,2,4,16,1440]{4,3,2,1,0:T(8,128)(2,1)S(1)}, bf16[8,2,4,16,1440]{4,3,2,1,0:T(8,128)(2,1)}, u32[]{:S(2)}) copy-start(bf16[8,2,4,16,1440]{4,3,2,1,0:T(8,128)(2,1)} %step_ref.5) | copy-start | bytes 8847364
  2.5 17.5 %collective-permute-start = (f32[4,16,1440]{2,1,0:T(8,128)}, f32[4,16,1440]{2,1,0:T(8,128)}, u32[]{:S(2)}, u32[]{:S(2)}) collective-permute-start(f32[4,16,1440]{2,1,0:T(8,128)} %slice_bitcast_fusion.1), channel_id=1, source_target_pairs={{16,0},{32,16},{48,32},{64,48},{80,64},{96,80},{112,96},{17,1},{33... | collective-permute-start | bytes 1105928 | tf_op jit(solution)/shard_map/ppermute | solution.py:21
  6.1 1.1 %copy-start.2 = (f32[2,4,16,1440]{3,2,1,0:T(8,128)S(1)}, f32[2,4,16,1440]{3,2,1,0:T(8,128)}, u32[]{:S(2)}) copy-start(f32[2,4,16,1440]{3,2,1,0:T(8,128)} %inc_ref.5) | copy-start | bytes 2211844
  7.2 1.0 %copy-start.4 = (f32[4,16,1440]{2,1,0:T(8,128)S(1)}, f32[4,16,1440]{2,1,0:T(8,128)}, u32[]{:S(2)}) copy-start(f32[4,16,1440]{2,1,0:T(8,128)} %lat_ref.5) | copy-start | bytes 1105924
  8.2 1.0 %copy-start.6 = (f32[4,16,1440]{2,1,0:T(8,128)S(1)}, f32[4,16,1440]{2,1,0:T(8,128)}, u32[]{:S(2)}) copy-start(f32[4,16,1440]{2,1,0:T(8,128)} %lon_ref.5) | copy-start | bytes 1105924
  9.2 1.1 %copy-start.9 = (f32[2,4,16,1440]{3,2,1,0:T(8,128)S(1)}, f32[2,4,16,1440]{3,2,1,0:T(8,128)}, u32[]{:S(2)}) copy-start(f32[2,4,16,1440]{3,2,1,0:T(8,128)} %forcing_ref.3) | copy-start | bytes 2211844
  11.8 8.1 %collective-permute-start.1 = (f32[8,4,1440]{2,1,0:T(4,128)}, f32[8,4,1440]{2,1,0:T(4,128)}, u32[]{:S(2)}, u32[]{:S(2)}) collective-permute-start(f32[8,4,1440]{2,1,0:T(4,128)} %edge.1), channel_id=1, source_target_pairs={{0,1},{1,2},{2,3},{3,4},{4,5},{5,6},{6,7},{7,8},{8,9},{9,10},{10,1... | collective-permute-start | bytes 552968 | tf_op jit(solution)/shard_map/ppermute | solution.py:21
  15.8 33.8 %copy-start.1 = (bf16[8,2,4,16,1440]{4,3,2,1,0:T(8,128)(2,1)S(1)}, bf16[8,2,4,16,1440]{4,3,2,1,0:T(8,128)(2,1)}, u32[]{:S(2)}) copy-start(bf16[8,2,4,16,1440]{4,3,2,1,0:T(8,128)(2,1)} %change_ref.5) | copy-start | bytes 8847364
  20.0 1.1 %copy-start.3 = (f32[2,4,16,1440]{3,2,1,0:T(8,128)S(1)}, f32[2,4,16,1440]{3,2,1,0:T(8,128)}, u32[]{:S(2)}) copy-start(f32[2,4,16,1440]{3,2,1,0:T(8,128)} %inc_ref.5) | copy-start | bytes 2211844
  21.1 1.0 %copy-start.7 = (f32[4,16,1440]{2,1,0:T(8,128)S(1)}, f32[4,16,1440]{2,1,0:T(8,128)}, u32[]{:S(2)}) copy-start(f32[4,16,1440]{2,1,0:T(8,128)} %lon_ref.5) | copy-start | bytes 1105924
  22.1 1.1 %copy-start.10 = (f32[2,4,16,1440]{3,2,1,0:T(8,128)S(1)}, f32[2,4,16,1440]{3,2,1,0:T(8,128)}, u32[]{:S(2)}) copy-start(f32[2,4,16,1440]{3,2,1,0:T(8,128)} %forcing_ref.3) | copy-start | bytes 2211844
  23.2 1.0 %copy-start.11 = (f32[4,16,1440]{2,1,0:T(8,128)S(1)}, f32[4,16,1440]{2,1,0:T(8,128)}, u32[]{:S(2)}) copy-start(f32[4,16,1440]{2,1,0:T(8,128)} %ew_ref.3) | copy-start | bytes 1105924
  24.2 0.8 copy-start.14
  25.1 0.8 copy-start.15
  25.9 0.8 copy-start.16
  45.6 14.7 %collective-permute-start.2 = (f32[4,16,1440]{2,1,0:T(8,128)S(1)}, f32[4,16,1440]{2,1,0:T(8,128)S(1)}, u32[]{:S(2)}, u32[]{:S(2)}) collective-permute-start(f32[4,16,1440]{2,1,0:T(8,128)S(1)} %slice_bitcast_fusion), channel_id=1, source_target_pairs={{0,16},{16,32},{32,48},{48,64},{64,80},{80,96},{96,112},{1,17},{17... | collective-permute-start | bytes 1105928 | tf_op jit(solution)/shard_map/ppermute | solution.py:21
  52.5 7.8 %collective-permute-start.3 = (f32[8,4,1440]{2,1,0:T(4,128)S(1)}, f32[8,4,1440]{2,1,0:T(4,128)S(1)}, u32[]{:S(2)}, u32[]{:S(2)}) collective-permute-start(f32[8,4,1440]{2,1,0:T(4,128)S(1)} %get-tuple-element.15), channel_id=1, source_target_pairs={{1,0},{2,1},{3,2},{4,3},{5,4},{6,5},{7,6},{8,7},{9,8},{10,9},{11,1... | collective-permute-start | bytes 552968 | tf_op jit(solution)/shard_map/ppermute | solution.py:21
  53.8 6.5 %copy-start.8 = (f32[4,16,1440]{2,1,0:T(8,128)S(1)}, f32[4,16,1440]{2,1,0:T(8,128)}, u32[]{:S(2)}) copy-start(f32[4,16,1440]{2,1,0:T(8,128)} %lon_ref.5) | copy-start | bytes 1105924
  53.8 6.5 %copy-start.12 = (f32[4,16,1440]{2,1,0:T(8,128)S(1)}, f32[4,16,1440]{2,1,0:T(8,128)}, u32[]{:S(2)}) copy-start(f32[4,16,1440]{2,1,0:T(8,128)} %ew_ref.3) | copy-start | bytes 1105924
  89.7 1.1 %copy-start.13 = (f32[2,4,16,1440]{3,2,1,0:T(8,128)S(1)}, f32[2,4,16,1440]{3,2,1,0:T(8,128)}, u32[]{:S(2)}) copy-start(f32[2,4,16,1440]{3,2,1,0:T(8,128)} %get-tuple-element.8.grad_ref) | copy-start | bytes 2211844

commit v2 on v0

v2 whole, which is shorter than its diff:
```python
import functools

import jax
import jax.numpy as jnp
from jax import lax
from jax.experimental import pallas as pl
from jax.experimental.pallas import tpu as pltpu
from jax.sharding import PartitionSpec as P

NSTEP = 4
LANES = 128
F32 = jnp.float32
BF16 = jnp.bfloat16
WHOLE = pl.BlockSpec(memory_space=pltpu.VMEM)
SCALAR = pl.BlockSpec(memory_space=pltpu.SMEM)
FAR = pl.BlockSpec(memory_space=pl.ANY)


def shifted(shard, axis, by):
    count = lax.axis_size(axis)
    pairs = [(i, i + by) for i in range(count) if 0 <= i + by < count]
    return lax.ppermute(shard, axis, pairs)


def west(x):
    return jnp.concatenate([x[:, -1:], x[:, :-1]], axis=1)


def east(x):
    return jnp.concatenate([x[:, 1:], x[:, :1]], axis=1)


def rows_of(x):
    return lax.broadcasted_iota(jnp.int32, x.shape, 0)


def params(mib):
    return pltpu.CompilerParams(vmem_limit_bytes=mib << 20)


def halves(x):
    high = x.astype(BF16)
    return high, (x - high.astype(F32)).astype(BF16)


def edge_kernel(*refs):
    sources, (following_ref, edge_ref), homes, sems = refs[:6], refs[6:8], refs[8:14], refs[14]
    copies = [
        pltpu.make_async_copy(source, home, sems.at[i])
        for i, (source, home) in enumerate(zip(sources, homes))
    ]
    copies.append(pltpu.make_async_copy(sources[0].at[0], following_ref, sems.at[len(copies)]))
    for copy in copies:
        copy.start()
    for copy in copies[:4]:
        copy.wait()
    inc_ref, forcing_ref, lat_ref, lon_ref = homes[:4]
    levels = lat_ref.shape[0]

    def one(j, _):
        sub, lev = j // levels, j % levels
        x, push = inc_ref[sub, lev, 8:], forcing_ref[sub, lev, 8:]
        lat, lon = lat_ref[lev, 8:], lon_ref[lev, 8:]
        rest = 1.0 - lat - lon
        for step in range(NSTEP):
            edge_ref[j, step : step + 1, :] = x[7:8, :]
            if step < NSTEP - 1:
                x = rest * x + lat * pltpu.roll(x, 1, 0) + lon * west(x) + push
        return 0

    lax.fori_loop(0, edge_ref.shape[0], one, 0)
    for copy in copies[4:]:
        copy.wait()


def pairs_kernel(step_ref, change_ref, out_ref, acc_ref):
    pairs, subs, levels, rows, longs = step_ref.shape
    acc_ref[...] = jnp.zeros_like(acc_ref)

    def one(j, _):
        sub, lev = j // levels, j % levels
        steps = step_ref[:, sub, lev].reshape(pairs * rows, longs)
        changes = change_ref[:, sub, lev].reshape(pairs * rows, longs)
        left = jnp.concatenate([steps, changes], axis=0)
        acc_ref[...] += lax.dot_general(
            left, changes, (((1,), (1,)), ((), ())), preferred_element_type=F32
        )
        return 0

    lax.fori_loop(0, subs * levels, one, 0)
    total = acc_ref[...]
    row = lax.broadcasted_iota(jnp.int32, total.shape, 0)
    col = lax.broadcasted_iota(jnp.int32, total.shape, 1)
    total = jnp.where(row % rows == col % rows, total, 0.0)
    sums = [
        jnp.sum(total[v * rows : (v + 1) * rows], axis=0, keepdims=True) for v in range(2 * pairs)
    ]
    out_ref[...] = jnp.concatenate(sums, axis=0)


SPLIT = 8
INNER = 512
EDGE = 192
OUTER = 256


def one_hot(first, count, cell):
    place = lax.broadcasted_iota(jnp.int16, (count, cell.shape[1]), 0) + jnp.int16(first)
    return jnp.where(place == cell, jnp.ones((), BF16), jnp.zeros((), BF16))


def four_rows(ref, k, low, tile):
    lanes = slice(tile * LANES, (tile + 1) * LANES)
    return [ref[k, lev, low : low + 4, lanes] for lev in range(ref.shape[1])]


def look_up(blocks, first, cell, lane, store):
    table = jnp.concatenate(halves(jnp.concatenate([b.T for b in blocks], axis=1)), axis=0)
    chunk = 256
    for start in range(0, cell.shape[1], chunk):
        part = slice(start, start + chunk)
        hot = one_hot(first, table.shape[1], cell[:, part])
        got = jnp.dot(table, hot, preferred_element_type=F32)
        got = got[:LANES] + got[LANES:]
        mine = lax.broadcasted_iota(jnp.int32, (LANES, chunk), 0) == lane[:, part]
        store(part, jnp.sum(jnp.where(mine, got, 0.0), axis=0, keepdims=True))


def inner_kernel(
    inc_ref,
    forcing_ref,
    lat_ref,
    lon_ref,
    index_ref,
    step_far,
    change_far,
    rows_ref,
    end_ref,
    gram_ref,
    state_ref,
    acc_ref,
    seen_ref,
    cell_ref,
    lane_ref,
    step_ref,
    change_ref,
    sems,
):
    subs, levels, rows, longs = inc_ref.shape
    copies = [
        pltpu.make_async_copy(step_far, step_ref, sems.at[0]),
        pltpu.make_async_copy(change_far, change_ref, sems.at[1]),
    ]
    for copy in copies:
        copy.start()
    tiles = -(-longs // LANES)
    state_ref[:, :, :, longs - longs % LANES :] = jnp.zeros(
        (subs * NSTEP, levels, rows, LANES), F32
    )
    for sub in range(subs):
        index = index_ref[sub]
        row = ((index.astype(F32) + 0.5) * (1.0 / longs)).astype(jnp.int32)
        lon = index - row * longs
        lev, lat = row // rows, row % rows
        tile, lane = lon // LANES, lon % LANES
        band = tile * 16 + lev * 4 + lat % 4
        cell = jnp.where(
            lat >= 8,
            tile * 32 + lev * 8 + lat - 8,
            jnp.where(
                lat < 4,
                INNER + band,
                jnp.where(tile < SPLIT, 384 + band, INNER + EDGE - SPLIT * 16 + band),
            ),
        )
        for step in range(NSTEP):
            k = sub * NSTEP + step
            cell_ref[k] = cell[step : step + 1]
            lane_ref[k] = lane[step : step + 1]
            rows_ref[1, k : k + 1, :] = cell[step : step + 1].astype(F32)
            rows_ref[2, k : k + 1, :] = lane[step : step + 1].astype(F32)

    def tangent(sub, lev):
        x = inc_ref[sub, lev]
        lat, lon, push = lat_ref[lev], lon_ref[lev], forcing_ref[sub, lev]
        rest = 1.0 - lat - lon
        for step in range(NSTEP):
            x = rest * x + lat * pltpu.roll(x, 1, 0) + lon * west(x) + push
            state_ref[sub * NSTEP + step, lev, :, :longs] = x
        end_ref[sub, lev] = x[8:]

    def gather(k):
        blocks = []
        for first in range(0, tiles, 4):
            part = [
                state_ref[k, :, 8:, t * LANES : (t + 1) * LANES].reshape(levels * 8, LANES)
                for t in range(first, first + 4)
            ]
            blocks.append(jnp.concatenate(part, axis=0))
        part = []
        for t in range(SPLIT):
            part += four_rows(state_ref, k, 4, t)
        blocks.append(jnp.concatenate(part, axis=0))

        def store(part, value):
            seen_ref[k, :, part] = value

        look_up(blocks, 0, cell_ref[k].astype(jnp.int16), lane_ref[k], store)

    def first(lev, _):
        tangent(0, lev)
        return 0

    lax.fori_loop(0, levels, first, 0)
    for sub in range(subs):

        def both(i, _, sub=sub):
            gather(sub * NSTEP + i)
            if sub + 1 < subs:
                tangent(sub + 1, i)
            return 0

        lax.fori_loop(0, NSTEP, both, 0, unroll=2)
    for k in range(subs * NSTEP):
        rows_ref[0, k : k + 1, :] = seen_ref[k]
    for copy in copies:
        copy.wait()
    pairs_kernel(step_ref, change_ref, gram_ref, acc_ref)


def outer_kernel(
    last_ref,
    inc_ref,
    forcing_ref,
    lat_ref,
    lon_ref,
    ew_ref,
    next_ref,
    above_ref,
    count_ref,
    value_far,
    weight_far,
    rows_ref,
    upper_ref,
    end_ref,
    sent_ref,
    edge_ref,
    inject_ref,
    dep_ref,
    state_ref,
    value_ref,
    weight_ref,
    seen_ref,
    cell_ref,
    lane_ref,
    dep_row,
    sems,
):
    subs, levels, _, longs = inc_ref.shape
    slots = value_ref.shape[2]
    tiles = -(-longs // LANES)
    copies = [
        pltpu.make_async_copy(value_far, value_ref, sems.at[0]),
        pltpu.make_async_copy(weight_far, weight_ref, sems.at[1]),
    ]
    for copy in copies:
        copy.start()
    state_ref[:, :, :, longs - longs % LANES :] = jnp.zeros((subs * NSTEP, levels, 8, LANES), F32)
    take_rows(rows_ref, cell_ref, lane_ref)

    def tangent(j, _):
        sub, lev = j // levels, j % levels
        x, push = inc_ref[sub, lev, :8], forcing_ref[sub, lev, :8]
        lat, lon = lat_ref[lev, :8], lon_ref[lev, :8]
        rest = 1.0 - lat - lon
        top = rows_of(x) == 0
        for step in range(NSTEP):
            above = jnp.where(top, above_ref[j, step : step + 1, :], pltpu.roll(x, 1, 0))
            x = rest * x + lat * above + lon * west(x) + push
            state_ref[sub * NSTEP + step, lev, :, :longs] = x
        end_ref[sub, lev] = x
        return 0

    lax.fori_loop(0, subs * levels, tangent, 0)
    sent_ref[:, :8] = end_ref[subs - 1]
    sent_ref[:, 8:] = upper_ref[subs - 1]

    def gather(k, _):
        part = []
        for t in range(tiles):
            part += four_rows(state_ref, k, 0, t)
        for t in range(SPLIT, tiles):
            part += four_rows(state_ref, k, 4, t)
        half = len(part) // 2
        blocks = [jnp.concatenate(part[:half], axis=0), jnp.concatenate(part[half:], axis=0)]

        def store(part, value):
            seen_ref[k, :, part] = value

        look_up(blocks, INNER, cell_ref[k].astype(jnp.int16), lane_ref[k], store)
        return 0

    lax.fori_loop(0, subs * NSTEP, gather, 0, unroll=2)

    slot = lax.broadcasted_iota(jnp.int32, (NSTEP, slots), 1)
    row = lax.broadcasted_iota(jnp.int32, (NSTEP, slots), 0)
    for copy in copies:
        copy.wait()
    for sub in range(subs):
        ks = range(sub * NSTEP, (sub + 1) * NSTEP)
        seen = rows_ref[0, ks.start : ks.stop, :]
        seen = seen + jnp.concatenate([seen_ref[k] for k in ks], axis=0)
        live = slot < 0
        for step in range(NSTEP):
            live = live | ((row == step) & (slot < count_ref[sub, step]))
        dep = jnp.where(live, weight_ref[sub] * (value_ref[sub] - seen), 0.0)
        dep_ref[ks.start : ks.stop, :] = dep
        for step in range(NSTEP):
            dep_row[ks[step]] = dep[step : step + 1]

    def scatter(k, _):
        cell = cell_ref[k].astype(jnp.int16)
        out = spread(one_hot(INNER, EDGE, cell), lane_ref[k], dep_row[k])
        store_four(inject_ref, k, 0, out, 0, tiles)
        return 0

    lax.fori_loop(0, subs * NSTEP, scatter, 0, unroll=2)

    for sub in range(subs):
        for lev in range(levels):
            j = sub * levels + lev
            later = next_ref[lev, :8] if sub == subs - 1 else inc_ref[sub + 1, lev, :8]
            d = ew_ref[lev, :8] * (later - end_ref[sub, lev])
            if sub == subs - 1:
                d = d * last_ref[0]
            lat, lon = lat_ref[lev, :8], lon_ref[lev, :8]
            rest = 1.0 - lat - lon
            for step in range(NSTEP - 1, -1, -1):
                d = d + inject_ref[sub * NSTEP + step, lev]
                part = lat * d
                edge_ref[j, step : step + 1, :] = part[:1, :]
                if step:
                    d = rest * d + pltpu.roll(part, 7, 0) + east(lon * d)


def spread(hot, lane, dep):
    high, low = halves(dep)
    mine = lax.broadcasted_iota(jnp.int16, (LANES, dep.shape[1]), 0) == lane.astype(jnp.int16)
    zero = jnp.zeros((), BF16)
    values = jnp.concatenate([jnp.where(mine, high, zero), jnp.where(mine, low, zero)], axis=0)
    out = lax.dot_general(hot, values, (((1,), (1,)), ((), ())), preferred_element_type=F32)
    return out[:, :LANES] + out[:, LANES:]


def take_rows(rows_ref, cell_ref, lane_ref):
    for k in range(rows_ref.shape[1]):
        cell_ref[k] = rows_ref[1, k : k + 1, :].astype(jnp.int32)
        lane_ref[k] = rows_ref[2, k : k + 1, :].astype(jnp.int32)


def store_tile(ref, k, lev, low, tile, x):
    longs = ref.shape[3]
    stop = min((tile + 1) * LANES, longs)
    ref[k, lev, low : low + x.shape[0], tile * LANES : stop] = x[:, : stop - tile * LANES]


def store_four(ref, k, low, out, first, stop):
    levels = ref.shape[1]
    for t in range(first, stop):
        for lev in range(levels):
            at = ((t - first) * levels + lev) * 4
            store_tile(ref, k, lev, low, t, out[at : at + 4])


def scatter_kernel(
    rows_ref, dep_ref, part_ref, lower_ref, upper_ref, cell_ref, lane_ref, dep_row
):
    count, levels, _, longs = lower_ref.shape
    take_rows(rows_ref, cell_ref, lane_ref)
    for k in range(count):
        dep_row[k] = dep_ref[k : k + 1, :]
    tiles = -(-longs // LANES)
    high = tiles * levels * 8

    def one(k, _):
        cell = cell_ref[k].astype(jnp.int16)
        hot = jnp.concatenate(
            [one_hot(0, INNER, cell), one_hot(INNER + EDGE, OUTER - EDGE, cell)], axis=0
        )
        out = spread(hot, lane_ref[k], dep_row[k])
        for t in range(tiles):
            for lev in range(levels):
                at = (t * levels + lev) * 8
                store_tile(upper_ref, k, lev, 0, t, out[at : at + 8])
        lower_ref[k, :, :4] = part_ref[k, :, :4]
        store_four(lower_ref, k, 4, out[high:], 0, tiles)
        return 0

    lax.fori_loop(0, count, one, 0, unroll=2)


def gradient_kernel(
    last_ref,
    inc_ref,
    lat_ref,
    lon_ref,
    ew_ref,
    next_ref,
    end_low_ref,
    end_high_ref,
    previous_ref,
    lower_ref,
    upper_ref,
    below_ref,
    gram_ref,
    step_ref,
    change_ref,
    grad_ref,
    stats_ref,
    dots_ref,
):
    subs, levels, rows, longs = inc_ref.shape
    pairs = step_ref.shape[0]
    count = subs * levels
    dots_ref[...] = jnp.zeros_like(dots_ref)

    def one(j, _):
        sub, lev = j // levels, j % levels
        ew = ew_ref[lev]
        final = sub == subs - 1
        later = jnp.where(final, next_ref[lev], inc_ref[jnp.minimum(sub + 1, subs - 1), lev])
        d = ew * (later - jnp.concatenate([end_low_ref[sub, lev], end_high_ref[sub, lev]], axis=0))
        d = d * jnp.where(final, last_ref[0], 1.0)
        lat, lon = lat_ref[lev], lon_ref[lev]
        rest = 1.0 - lat - lon
        bottom = rows_of(d) == rows - 1
        for step in range(NSTEP - 1, -1, -1):
            k = sub * NSTEP + step
            d = d + jnp.concatenate([lower_ref[k, lev], upper_ref[k, lev]], axis=0)
            part = lat * d
            below = jnp.where(
                bottom, below_ref[j, step : step + 1, :], pltpu.roll(part, rows - 1, 0)
            )
            d = rest * d + below + east(lon * d)
        before = jnp.maximum(sub - 1, 0)
        before = jnp.concatenate([end_low_ref[before, lev], end_high_ref[before, lev]], axis=0)
        earlier = jnp.where(sub == 0, previous_ref[lev], before)
        g = ew * (inc_ref[sub, lev] - earlier) - d
        grad_ref[sub, lev] = g
        for i in range(pairs):
            for which, ref in enumerate((step_ref, change_ref)):
                dots_ref[which * pairs + i] += fold(g * ref[i, sub, lev].astype(F32))
        return 0

    lax.fori_loop(0, count, one, 0)
    sums = [jnp.sum(dots_ref[v], axis=0, keepdims=True) for v in range(2 * pairs)]
    sums = jnp.concatenate(sums, axis=0)
    dots = jnp.sum(sums, axis=1, keepdims=True)
    raw = gram_ref[...]
    row = lax.broadcasted_iota(jnp.int32, raw.shape, 0)
    col = lax.broadcasted_iota(jnp.int32, raw.shape, 1)
    group = col // rows
    here = col % rows == row
    out = jnp.zeros((1, raw.shape[1]), F32)
    for c in range(pairs):
        part = jnp.sum(jnp.where(group == c, raw, 0.0), axis=1, keepdims=True)
        out += jnp.sum(jnp.where(here & (group == c), part, 0.0), axis=0, keepdims=True)
    stats_ref[0:1, :] = out
    stats_ref[1:2, :] = jnp.sum(jnp.where(here, dots, 0.0), axis=0, keepdims=True)


def fold(x):
    longs = x.shape[1]
    whole = longs - longs % LANES
    x = x[:8] + x[8:]
    out = x[:, :LANES]
    for first in range(LANES, whole, LANES):
        out = out + x[:, first : first + LANES]
    if whole < longs:
        tail = jnp.concatenate(
            [x[:, whole:], jnp.zeros((8, LANES - (longs - whole)), F32)], axis=1
        )
        out = out + tail
    return out


def direction_kernel(
    stats_ref, grad_ref, step_ref, change_ref, grad_out, direction_out, coef_ref, out_ref, sems
):
    pairs, subs, levels, _, _ = step_ref.shape
    both = 2 * pairs
    count = subs * levels
    handed = pltpu.make_async_copy(grad_ref, grad_out, sems.at[count])
    handed.start()
    gram = jnp.sum(stats_ref[:, 0, :], axis=0, keepdims=True)
    dots = jnp.sum(stats_ref[:, 1, :], axis=0, keepdims=True)
    shape = (both, LANES)
    row = lax.broadcasted_iota(jnp.int32, shape, 0)
    col = lax.broadcasted_iota(jnp.int32, shape, 1)
    group, inner = col // both, col % both
    gram = jnp.broadcast_to(gram, shape)
    dots = jnp.broadcast_to(dots, shape)

    def column(mask, x):
        return jnp.sum(jnp.where(mask, x, 0.0), axis=1, keepdims=True)

    dots = column((inner == row) & (group == 0), dots)
    by_change = [column((inner == row) & (group == c), gram) for c in range(pairs)]
    by_step = [column((group == row) & (inner == i), gram)[:pairs] for i in range(pairs)]
    diagonal = column((group == row) & (inner == row), gram)[:pairs]
    rho = 1.0 / diagonal
    with_step, with_change = dots[:pairs], dots[pairs:]
    alphas = [None] * pairs
    for i in range(pairs - 1, -1, -1):
        alphas[i] = rho[i : i + 1] * with_step[i : i + 1]
        with_step = with_step - alphas[i] * by_change[i][:pairs]
        with_change = with_change - alphas[i] * by_change[i][pairs:]
    gamma = diagonal[pairs - 1 : pairs] / by_change[pairs - 1][both - 1 : both]
    with_change = gamma * with_change
    coef_ref[both] = jnp.broadcast_to(gamma, (8, LANES))
    for i in range(pairs):
        beta = rho[i : i + 1] * with_change[i : i + 1]
        rise = alphas[i] - beta
        with_change = with_change + rise * by_step[i]
        coef_ref[i] = jnp.broadcast_to(rise, (8, LANES))
        coef_ref[pairs + i] = jnp.broadcast_to(-gamma * alphas[i], (8, LANES))


    def copy(j):
        sub, lev = j // levels, j % levels
        return pltpu.make_async_copy(
            out_ref.at[sub, lev], direction_out.at[sub, lev], sems.at[j]
        )

    def one(j, _):
        sub, lev = j // levels, j % levels
        total = coef_ref[both][:1, :1] * grad_ref[sub, lev]
        for i in range(pairs):
            total += coef_ref[i][:1, :1] * step_ref[i, sub, lev].astype(F32)
            total += coef_ref[pairs + i][:1, :1] * change_ref[i, sub, lev].astype(F32)
        out_ref[sub, lev] = total
        copy(j).start()
        return 0

    lax.fori_loop(0, count, one, 0)
    for j in range(count):
        copy(j).wait()
    handed.wait()


def on_device(
    increment,
    forcing,
    lat_courant,
    lon_courant,
    error_weight,
    site_index,
    site_count,
    site_value,
    site_weight,
    pair_step,
    pair_change,
):
    subs, levels, rows, longs = increment.shape
    pairs = pair_step.shape[0]
    slots = site_index.shape[2]
    count = subs * levels
    wide = -(-longs // LANES) * LANES
    devices = lax.axis_size("tm") * lax.axis_size("space")
    last = jnp.where(lax.axis_index("tm") == lax.axis_size("tm") - 1, 0.0, 1.0)
    last = last.astype(F32).reshape(1)

    def like(x):
        return pltpu.VMEM(x.shape, x.dtype)

    def floats(*shape):
        return pltpu.VMEM(shape, F32)

    def cost(flops):
        return pl.CostEstimate(flops=flops, bytes_accessed=1 << 20, transcendentals=0)

    def far(*arrays):
        return [pltpu.with_memory_space_constraint(x, pltpu.HBM) for x in arrays]

    arguments = (increment, forcing, lat_courant, lon_courant, error_weight, site_index)
    following, edge, inc, push, lat, lon, ew, index = pl.pallas_call(
        edge_kernel,
        in_specs=[FAR] * len(arguments),
        out_specs=[WHOLE] * (2 + len(arguments)),
        out_shape=[floats(levels, rows, longs), floats(count, NSTEP, longs)]
        + [like(x) for x in arguments],
        scratch_shapes=[pltpu.SemaphoreType.DMA((len(arguments) + 1,))],
        compiler_params=params(16),
        name="edge",
    )(*far(*arguments))
    above = shifted(edge, "space", 1)
    following = shifted(following, "tm", -1)

    row_shape = (subs * NSTEP, 1, slots)
    row_scratch = [
        pltpu.VMEM(row_shape, F32),
        pltpu.VMEM(row_shape, jnp.int32),
        pltpu.VMEM(row_shape, jnp.int32),
    ]
    rows_of_slots, end_high, gram = pl.pallas_call(
        inner_kernel,
        in_specs=[WHOLE] * 5 + [FAR] * 2,
        out_specs=[WHOLE] * 3,
        out_shape=[
            floats(3, subs * NSTEP, slots),
            floats(subs, levels, 8, longs),
            floats(2 * pairs, pairs * rows),
        ],
        scratch_shapes=[
            pltpu.VMEM((subs * NSTEP, levels, rows, wide), F32),
            pltpu.VMEM((2 * pairs * rows, pairs * rows), F32),
        ]
        + row_scratch
        + [
            pltpu.VMEM(pair_step.shape, BF16),
            pltpu.VMEM(pair_step.shape, BF16),
            pltpu.SemaphoreType.DMA((2,)),
        ],
        compiler_params=params(28),
        cost_estimate=cost(8 * 10**9),
        name="inner",
    )(inc, push, lat, lon, index, *far(pair_step, pair_change))

    end_low, sent, edge, part, dep = pl.pallas_call(
        outer_kernel,
        in_specs=[SCALAR] + [WHOLE] * 7 + [SCALAR] + [FAR] * 2 + [WHOLE] * 2,
        out_specs=[WHOLE] * 5,
        out_shape=[
            floats(subs, levels, 8, longs),
            floats(levels, rows, longs),
            floats(count, NSTEP, longs),
            floats(subs * NSTEP, levels, 8, longs),
            floats(subs * NSTEP, slots),
        ],
        scratch_shapes=[
            pltpu.VMEM((subs * NSTEP, levels, 8, wide), F32),
            pltpu.VMEM(site_value.shape, F32),
            pltpu.VMEM(site_value.shape, F32),
        ]
        + row_scratch
        + [pltpu.VMEM(row_shape, F32), pltpu.SemaphoreType.DMA((2,))],
        compiler_params=params(24),
        cost_estimate=cost(5 * 10**9),
        name="outer",
    )(
        last,
        inc,
        push,
        lat,
        lon,
        ew,
        following,
        above,
        site_count.reshape(subs, NSTEP),
        *far(site_value, site_weight),
        rows_of_slots,
        end_high,
    )
    below = shifted(edge, "space", -1)
    previous = shifted(sent, "tm", 1)

    lower, upper = pl.pallas_call(
        scatter_kernel,
        in_specs=[WHOLE] * 3,
        out_specs=[WHOLE] * 2,
        out_shape=[floats(subs * NSTEP, levels, 8, longs)] * 2,
        scratch_shapes=row_scratch[1:] + row_scratch[:1],
        compiler_params=params(24),
        cost_estimate=cost(6 * 10**9),
        name="scatter",
    )(rows_of_slots, dep, part)

    gradient, stats = pl.pallas_call(
        gradient_kernel,
        in_specs=[SCALAR] + [WHOLE] * 14,
        out_specs=[WHOLE] * 2,
        out_shape=[like(increment), floats(2, LANES)],
        scratch_shapes=[pltpu.VMEM((2 * pairs, 8, LANES), F32)],
        compiler_params=params(16),
        name="gradient",
    )(
        last,
        inc,
        lat,
        lon,
        ew,
        following,
        end_low,
        end_high,
        previous,
        lower,
        upper,
        below,
        gram,
        pair_step,
        pair_change,
    )

    stats = jnp.broadcast_to(stats[None], (devices,) + stats.shape)
    stats = lax.all_to_all(stats, ("tm", "space"), 0, 0)

    return pl.pallas_call(
        direction_kernel,
        in_specs=[WHOLE] * 4,
        out_specs=[FAR] * 2,
        out_shape=[jax.ShapeDtypeStruct(increment.shape, F32)] * 2,
        scratch_shapes=[
            pltpu.VMEM((2 * pairs + 1, 8, LANES), F32),
            pltpu.VMEM(increment.shape, F32),
            pltpu.SemaphoreType.DMA((count + 1,)),
        ],
        compiler_params=params(16),
        name="direction",
    )(stats, gradient, pair_step, pair_change)


def solution(mesh):
    return jax.shard_map(
        on_device,
        mesh=mesh,
        in_specs=(
            P("tm", None, "space", None),
            P("tm", None, "space", None),
            P(None, "space", None),
            P(None, "space", None),
            P(None, "space", None),
            P("tm", None, "space"),
            P("tm", None, "space"),
            P("tm", None, "space"),
            P("tm", None, "space"),
            P(None, "tm", None, "space", None),
            P(None, "tm", None, "space", None),
        ),
        out_specs=(P("tm", None, "space", None), P("tm", None, "space", None)),
        check_vma=False,
    )
```

time: 1420 us -> 74.1 us (0.05)
  blocking collectives: 1030 us -> 20.2 us
  local copies, waits for them, and re-layouts: 174 us -> 1.64 us
  other arithmetic: 147 us -> 0 us
  Pallas kernels: 0 us -> 38.9 us
  starting transfers between devices: 30 us -> 12.3 us
  between operations: 18.3 us -> 0.78 us
    psum x16 -> x0, blocking collectives: 1030 us -> none  [the longest x8 507 us: on_device(): beta = 1.0 / stats[i] * lax.psum(local_dot, ('tm', 'space'))]
    gather x8 -> x0, local copies, waits for them, and re-layouts: 140 us -> none  [on_device(): jnp.take_along_axis(state.reshape(subs, total), site_index[:, step], axis=1)]
    unnamed x14 -> x0, other arithmetic: 89.9 us -> none
    reduce_sum x16 -> x0, other arithmetic: 40 us -> none  [the longest x8 19.6 us: on_device(): local_dot = jnp.sum(pair_change[i].astype(jnp.float32) * result)]
    pallas_call x0 -> x6, Pallas kernels: none -> 38.9 us  [the longest x1 11.3 us: on_device(): pl.pallas_call(outer_kernel, in_specs=[SCALAR] + [WHOLE] * 7 + [SCALAR] +...]
    all_to_all x0 -> x1, blocking collectives: none -> 20.2 us  [on_device(): stats = lax.all_to_all(stats, ('tm', 'space'), 0, 0)]
    ppermute x10 -> x4, starting transfers between devices: 30 us -> 12.3 us  [shifted(): return lax.ppermute(shard, axis, pairs)]
    slice x28 -> x0, local copies, waits for them, and re-layouts: 14.5 us -> none  [the longest x4 3.94 us: adjoint(): below = jnp.concatenate([lat_part[:, :, 1:, :], bottom], axis=2)]
  transfers between devices with their start and end apart: 10 -> 4, of which waited for: 5 -> 0; matrix products, arithmetic and copies ran while one was open for 18% -> 0% of each run, Pallas kernels for 0% -> 22%
where the time goes in v2:
time: 74.1 us; the launch traced here: 73.9 us
  Pallas kernels  38.9 us (52%)
  blocking collectives  20.2 us (27%)
  starting transfers between devices  12.3 us (17%)
  local copies, waits for them, and re-layouts  1.64 us (2%)
  between operations  0.78 us (1%)
    all_to_all x1, blocking collectives, on_device(): stats = lax.all_to_all(stats, ('tm', 'space'), 0, 0)  20.2 us
    ppermute x4, starting transfers between devices, shifted(): return lax.ppermute(shard, axis, pairs)  12.3 us
    pallas_call x1, Pallas kernels, on_device(): pl.pallas_call(outer_kernel, in_specs=[SCALAR] + [WHOLE] * 7 + [SCALAR] +...  11.3 us
    pallas_call x1, Pallas kernels, on_device(): pl.pallas_call(inner_kernel, in_specs=[WHOLE] * 5 + [FAR] * 2, out_specs=...  10.6 us
    pallas_call x1, Pallas kernels, on_device(): pl.pallas_call(scatter_kernel, in_specs=[WHOLE] * 3, out_specs=[WHOLE] *...  5.72 us
    pallas_call x1, Pallas kernels, on_device(): pl.pallas_call(edge_kernel, in_specs=[FAR] * len(arguments), out_specs=[W...  4.55 us
    pallas_call x1, Pallas kernels, on_device(): pl.pallas_call(gradient_kernel, in_specs=[SCALAR] + [WHOLE] * 14, out_spe...  4.08 us
    pallas_call x1, Pallas kernels, on_device(): pl.pallas_call(direction_kernel, in_specs=[WHOLE] * 4, out_specs=[FAR] *...  2.67 us
  transfers between devices with their start and end apart: 4, of which 0 were waited for; matrix products, arithmetic and copies ran while one was open for 0% of the time, Pallas kernels for 22%

profile of v2, /device:TPU:1, one launch (start us, length us, event | category | flops | bytes accessed | tf_op | source)
XLA Modules:
  0.0 73.9 jit_solution(1914756056572344407)
XLA Ops:
  0.6 4.6 %edge.1 = (f32[4,16,1440]{2,1,0:T(8,128)}, f32[8,4,1440]{2,1,0:T(4,128)}, f32[2,4,16,1440]{3,2,1,0:T(8,128)S(1)}, f32[2,4,16,1440]{3,2,1,0:T(8,128)S(1)}, f32[4,...) custom-call(f32[2,4,16,1440]{3,2,1,0:T(8,128)} %refs_0_.1, ...), custom_call_target="tpu_custom_call" | custom-call | tf_op jit(solution)/shard_map/edge/pallas_call | solution.py:586
  5.2 4.7 %collective-permute-start.1 = (f32[8,4,1440]{2,1,0:T(4,128)}, f32[8,4,1440]{2,1,0:T(4,128)}, u32[]{:S(2)}, u32[]{:S(2)}) collective-permute-start(f32[8,4,1440]{2,1,0:T(4,128)} %get-tuple-element.28), channel_id=1, source_target_pairs={{0,1},{1,2},{2,3},{3,4},{4,5},{5,6},{6,7},{7,8},{8,9},{9,10},{10,1... | collective-permute-start | bytes 552968 | tf_op jit(solution)/shard_map/ppermute | solution.py:22
  9.9 2.9 %collective-permute-start = (f32[4,16,1440]{2,1,0:T(8,128)}, f32[4,16,1440]{2,1,0:T(8,128)S(1)}, u32[]{:S(2)}, u32[]{:S(2)}) collective-permute-start(f32[4,16,1440]{2,1,0:T(8,128)} %get-tuple-element.26), channel_id=1, source_target_pairs={{16,0},{32,16},{48,32},{64,48},{80,64},{96,80},{112,96},{17,1},{33... | collective-permute-start | bytes 1105928 | tf_op jit(solution)/shard_map/ppermute | solution.py:22
  12.8 0.0 copy-start.2
  12.8 10.6 %inner.1 = (f32[3,8,2048]{2,1,0:T(8,128)S(1)}, f32[2,4,8,1440]{3,2,1,0:T(8,128)S(1)}, f32[16,128]{1,0:T(8,128)S(1)}) custom-call(f32[2,4,16,1440]{3,2,1,0:T(8,128)S(1)} %get-tuple-element.22.inc_ref, f32[2,4,16,1440]{3,2,1,0:T(8,128)S(1)} %get-tuple-element.27.forcing_ref, f32[4,16,1440]{2,1,0:T(8,128)S(1)} %get-tuple-element.23.lat_ref, ...), custom_call_target="tpu_custom_call" | custom-call | flops 8000000000 | bytes 1048576 | tf_op jit(solution)/shard_map/inner/pallas_call | solution.py:605
  23.4 0.0 copy-start.3
  23.4 0.7 copy-done.3
  24.1 0.0 collective-permute-done.1.above_ref
  24.1 0.0 collective-permute-done.next_ref
  24.1 0.0 copy-done.2
  24.1 0.0 copy-start.4
  24.1 0.9 %copy-done.4 = f32[3,8,2048]{2,1,0:T(8,128)S(1)} copy-done((f32[3,8,2048]{2,1,0:T(8,128)S(1)}, f32[3,8,2048]{2,1,0:T(8,128)}, u32[]{:S(2)}) %copy-start.4) | copy-done | bytes 196632
  25.0 11.3 %outer.1 = (f32[2,4,8,1440]{3,2,1,0:T(8,128)S(1)}, f32[4,16,1440]{2,1,0:T(8,128)S(1)}, f32[8,4,1440]{2,1,0:T(4,128)S(1)}, f32[8,4,8,1440]{3,2,1,0:T(8,128)S(1)}, f32[8,2048]{1,0:T(8,128)S(1)}) custom-call(f32[1]{0:T(128)} %bitcast.last_ref, f32[2,4,16,1440]{3,2,1,0:T(8,128)S(1)} %get-tuple-element.22.inc_ref, ...), custom_call_target="tpu_custom_call" | custom-call | flops 5000000000 | bytes 1048576 | tf_op jit(solution)/shard_map/outer/pallas_call | solution.py:629
  36.3 1.3 %collective-permute-start.3 = (f32[8,4,1440]{2,1,0:T(4,128)S(1)}, f32[8,4,1440]{2,1,0:T(4,128)S(1)}, u32[]{:S(2)}, u32[]{:S(2)}) collective-permute-start(f32[8,4,1440]{2,1,0:T(4,128)S(1)} %get-tuple-element.38), channel_id=1, source_target_pairs={{1,0},{2,1},{3,2},{4,3},{5,4},{6,5},{7,6},{8,7},{9,8},{10,9},{11,1... | collective-permute-start | bytes 552968 | tf_op jit(solution)/shard_map/ppermute | solution.py:22
  37.6 3.4 %collective-permute-start.2 = (f32[4,16,1440]{2,1,0:T(8,128)S(1)}, f32[4,16,1440]{2,1,0:T(8,128)S(1)}, u32[]{:S(2)}, u32[]{:S(2)}) collective-permute-start(f32[4,16,1440]{2,1,0:T(8,128)S(1)} %get-tuple-element.33), channel_id=1, source_target_pairs={{0,16},{16,32},{32,48},{48,64},{64,80},{80,96},{96,112},{1,17},{17... | collective-permute-start | bytes 1105928 | tf_op jit(solution)/shard_map/ppermute | solution.py:22
  41.0 0.0 copy-start
  41.1 0.0 copy-start.1
  41.1 5.7 %scatter.1 = (f32[8,4,8,1440]{3,2,1,0:T(8,128)S(1)}, f32[8,4,8,1440]{3,2,1,0:T(8,128)S(1)}) custom-call(f32[3,8,2048]{2,1,0:T(8,128)S(1)} %copy-done.4, f32[8,2048]{1,0:T(8,128)S(1)} %get-tuple-element.34.dep_ref, f32[8,4,8,1440]{3,2,1,0:T(8,128)S(1)} %get-tuple-element.35.part_ref), custom_call_target="tpu_custom_call" | custom-call | flops 6000000000 | bytes 1048576 | tf_op jit(solution)/shard_map/scatter/pallas_call | solution.py:667
  46.8 0.0 collective-permute-done.3.below_ref
  46.8 0.0 collective-permute-done.2.previous_ref
  46.8 0.0 copy-done
  46.8 0.0 copy-done.1
  46.8 4.1 %gradient.1 = (f32[2,4,16,1440]{3,2,1,0:T(8,128)S(1)}, f32[2,128]{1,0:T(2,128)S(1)}) custom-call(f32[1]{0:T(128)} %bitcast.last_ref, f32[2,4,16,1440]{3,2,1,0:T(8,128)S(1)} %get-tuple-element.22.inc_ref, f32[4,16,1440]{2,1,0:T(8,128)S(1)} %get-tuple-element.23.lat_ref, f32[4,16,1440]{2,1,0:T(8,128)S(1)} %get-tuple-element.24.lon_ref, ...), custom_call_target="tpu_custom_call" | custom-call | tf_op jit(solution)/shard_map/gradient/pallas_call | solution.py:678
  51.0 20.2 %all_to_all.5.stats_ref = f32[128,2,128]{2,1,0:T(2,128)S(1)} all-to-all(f32[128,2,128]{2,1,0:T(2,128)S(1)} %broadcast_in_dim.2), channel_id=1, replica_groups=mesh['tm'=8,'space'=16] {'tm','space'}, dimensions={0} | all-to-all | bytes 262144 | tf_op jit(solution)/shard_map/all_to_all | solution.py:705
  71.2 2.7 %direction.1 = (f32[2,4,16,1440]{3,2,1,0:T(8,128)}, f32[2,4,16,1440]{3,2,1,0:T(8,128)}) custom-call(f32[128,2,128]{2,1,0:T(2,128)S(1)} %all_to_all.5.stats_ref, f32[2,4,16,1440]{3,2,1,0:T(8,128)S(1)} %get-tuple-element.41.grad_ref, bf16[8,2,4,16,1440]{4,3,2,1,0:T(8,128)(2,1)S(1)} %copy-done, bf16[8,2,4,16,1440]{4,3,2,1,0:T(8,128)(2,1)S(1)} %copy-done.1), custom_call_target="tpu_custom_call" | custom-call | tf_op jit(solution)/shard_map/direction/pallas_call | solution.py:707
  (1 shorter events, 0.0 us)
Async XLA Ops:
  5.2 18.9 %collective-permute-start.1 = (f32[8,4,1440]{2,1,0:T(4,128)}, f32[8,4,1440]{2,1,0:T(4,128)}, u32[]{:S(2)}, u32[]{:S(2)}) collective-permute-start(f32[8,4,1440]{2,1,0:T(4,128)} %get-tuple-element.28), channel_id=1, source_target_pairs={{0,1},{1,2},{2,3},{3,4},{4,5},{5,6},{6,7},{7,8},{8,9},{9,10},{10,1... | collective-permute-start | bytes 552968 | tf_op jit(solution)/shard_map/ppermute | solution.py:22
  9.9 14.1 %collective-permute-start = (f32[4,16,1440]{2,1,0:T(8,128)}, f32[4,16,1440]{2,1,0:T(8,128)S(1)}, u32[]{:S(2)}, u32[]{:S(2)}) collective-permute-start(f32[4,16,1440]{2,1,0:T(8,128)} %get-tuple-element.26), channel_id=1, source_target_pairs={{16,0},{32,16},{48,32},{64,48},{80,64},{96,80},{112,96},{17,1},{33... | collective-permute-start | bytes 1105928 | tf_op jit(solution)/shard_map/ppermute | solution.py:22
  12.8 11.3 %copy-start.2 = (s32[2,4,1]{1,2,0:T(1,128)S(1)}, s32[2,4,1]{1,2,0:T(1,128)}, u32[]{:S(2)}) copy-start(s32[2,4,1]{1,2,0:T(1,128)} %param.17) | copy-start | bytes 100
  23.4 0.7 copy-start.3
  24.1 0.9 %copy-start.4 = (f32[3,8,2048]{2,1,0:T(8,128)S(1)}, f32[3,8,2048]{2,1,0:T(8,128)}, u32[]{:S(2)}) copy-start(f32[3,8,2048]{2,1,0:T(8,128)} %copy-done.3) | copy-start | bytes 589828
  36.3 10.5 %collective-permute-start.3 = (f32[8,4,1440]{2,1,0:T(4,128)S(1)}, f32[8,4,1440]{2,1,0:T(4,128)S(1)}, u32[]{:S(2)}, u32[]{:S(2)}) collective-permute-start(f32[8,4,1440]{2,1,0:T(4,128)S(1)} %get-tuple-element.38), channel_id=1, source_target_pairs={{1,0},{2,1},{3,2},{4,3},{5,4},{6,5},{7,6},{8,7},{9,8},{10,9},{11,1... | collective-permute-start | bytes 552968 | tf_op jit(solution)/shard_map/ppermute | solution.py:22
  37.6 9.2 %collective-permute-start.2 = (f32[4,16,1440]{2,1,0:T(8,128)S(1)}, f32[4,16,1440]{2,1,0:T(8,128)S(1)}, u32[]{:S(2)}, u32[]{:S(2)}) collective-permute-start(f32[4,16,1440]{2,1,0:T(8,128)S(1)} %get-tuple-element.33), channel_id=1, source_target_pairs={{0,16},{16,32},{32,48},{48,64},{64,80},{80,96},{96,112},{1,17},{17... | collective-permute-start | bytes 1105928 | tf_op jit(solution)/shard_map/ppermute | solution.py:22
  41.0 5.8 %copy-start = (bf16[8,2,4,16,1440]{4,3,2,1,0:T(8,128)(2,1)S(1)}, bf16[8,2,4,16,1440]{4,3,2,1,0:T(8,128)(2,1)}, u32[]{:S(2)}) copy-start(bf16[8,2,4,16,1440]{4,3,2,1,0:T(8,128)(2,1)} %step_ref.3) | copy-start | bytes 8847364
  41.1 5.8 %copy-start.1 = (bf16[8,2,4,16,1440]{4,3,2,1,0:T(8,128)(2,1)S(1)}, bf16[8,2,4,16,1440]{4,3,2,1,0:T(8,128)(2,1)}, u32[]{:S(2)}) copy-start(bf16[8,2,4,16,1440]{4,3,2,1,0:T(8,128)(2,1)} %change_ref.3) | copy-start | bytes 8847364

commit v3 on v2

--- a/solution.py
+++ b/solution.py
@@ -45,11 +45,18 @@
 
 def edge_kernel(*refs):
     sources, (following_ref, edge_ref), homes, sems = refs[:6], refs[6:8], refs[8:14], refs[14]
+    def lower(ref):
+        return ref.at[:, :, 8:] if len(ref.shape) == 4 else ref.at[:, 8:]
+
+    def upper(ref):
+        return ref.at[:, :, :8] if len(ref.shape) == 4 else ref.at[:, :8]
+
+    pieces = [(lower(source), lower(home)) for source, home in zip(sources[:4], homes[:4])]
+    pieces += [(upper(source), upper(home)) for source, home in zip(sources[:4], homes[:4])]
+    pieces += list(zip(sources[4:], homes[4:])) + [(sources[0].at[0], following_ref)]
     copies = [
-        pltpu.make_async_copy(source, home, sems.at[i])
-        for i, (source, home) in enumerate(zip(sources, homes))
+        pltpu.make_async_copy(source, home, sems.at[i]) for i, (source, home) in enumerate(pieces)
     ]
-    copies.append(pltpu.make_async_copy(sources[0].at[0], following_ref, sems.at[len(copies)]))
     for copy in copies:
         copy.start()
     for copy in copies[:4]:
@@ -68,34 +75,48 @@
                 x = rest * x + lat * pltpu.roll(x, 1, 0) + lon * west(x) + push
         return 0
 
-    lax.fori_loop(0, edge_ref.shape[0], one, 0)
+    lax.fori_loop(0, edge_ref.shape[0], one, 0, unroll=4)
     for copy in copies[4:]:
         copy.wait()
 
 
-def pairs_kernel(step_ref, change_ref, out_ref, acc_ref):
-    pairs, subs, levels, rows, longs = step_ref.shape
-    acc_ref[...] = jnp.zeros_like(acc_ref)
-
-    def one(j, _):
-        sub, lev = j // levels, j % levels
-        steps = step_ref[:, sub, lev].reshape(pairs * rows, longs)
-        changes = change_ref[:, sub, lev].reshape(pairs * rows, longs)
-        left = jnp.concatenate([steps, changes], axis=0)
-        acc_ref[...] += lax.dot_general(
-            left, changes, (((1,), (1,)), ((), ())), preferred_element_type=F32
-        )
-        return 0
-
-    lax.fori_loop(0, subs * levels, one, 0)
-    total = acc_ref[...]
+def pair_products(step_ref, change_ref, acc_ref, j):
+    pairs, _, levels, rows, longs = step_ref.shape
+    sub, lev = j // levels, j % levels
+    steps = step_ref[:, sub, lev].reshape(pairs * rows, longs)
+    changes = change_ref[:, sub, lev].reshape(pairs * rows, longs)
+    both = jnp.concatenate([steps, changes], axis=0)
+    acc_ref[...] += lax.dot_general(
+        changes, both, (((1,), (1,)), ((), ())), preferred_element_type=F32
+    )
+
+
+def pair_sums(acc_ref, rows, out_ref):
+    total = acc_ref[...].T
     row = lax.broadcasted_iota(jnp.int32, total.shape, 0)
     col = lax.broadcasted_iota(jnp.int32, total.shape, 1)
     total = jnp.where(row % rows == col % rows, total, 0.0)
     sums = [
-        jnp.sum(total[v * rows : (v + 1) * rows], axis=0, keepdims=True) for v in range(2 * pairs)
+        jnp.sum(total[first : first + rows], axis=0, keepdims=True)
+        for first in range(0, total.shape[0], rows)
     ]
-    out_ref[...] = jnp.concatenate(sums, axis=0)
+    sums = jnp.concatenate(sums, axis=0)
+    row, group, inner = lane_places(sums.shape)
+    out = jnp.zeros(sums.shape, F32)
+    for c in range(sums.shape[1] // rows):
+        part = jnp.sum(jnp.where(group == c, sums, 0.0), axis=1, keepdims=True)
+        out = jnp.where((group == c) & (inner == row), part, out)
+    out_ref[...] = out
+
+
+def lane_places(shape):
+    row = lax.broadcasted_iota(jnp.int32, shape, 0)
+    col = lax.broadcasted_iota(jnp.int32, shape, 1)
+    return row, col // shape[0], col % shape[0]
+
+
+WITH_CHANGE = 5
+WITH_STEP = 6
 
 
 SPLIT = 8
@@ -137,19 +158,20 @@
     rows_ref,
     end_ref,
     gram_ref,
+    step_ref,
+    change_ref,
     state_ref,
     acc_ref,
     seen_ref,
     cell_ref,
     lane_ref,
-    step_ref,
-    change_ref,
     sems,
 ):
     subs, levels, rows, longs = inc_ref.shape
     copies = [
-        pltpu.make_async_copy(step_far, step_ref, sems.at[0]),
-        pltpu.make_async_copy(change_far, change_ref, sems.at[1]),
+        pltpu.make_async_copy(far.at[i], near.at[i], sems.at[which, i])
+        for i in range(step_ref.shape[0])
+        for which, (far, near) in enumerate(((step_far, step_ref), (change_far, change_ref)))
     ]
     for copy in copies:
         copy.start()
@@ -211,21 +233,26 @@
         tangent(0, lev)
         return 0
 
-    lax.fori_loop(0, levels, first, 0)
-    for sub in range(subs):
-
-        def both(i, _, sub=sub):
-            gather(sub * NSTEP + i)
-            if sub + 1 < subs:
-                tangent(sub + 1, i)
-            return 0
-
-        lax.fori_loop(0, NSTEP, both, 0, unroll=2)
+    lax.fori_loop(0, levels, first, 0, unroll=2)
+    acc_ref[...] = jnp.zeros_like(acc_ref)
+
+    count = subs * levels
+    for i in range(NSTEP // 2):
+        gather(i)
+        tangent(1, 2 * i)
+        tangent(1, 2 * i + 1)
+    for copy in copies:
+        copy.wait()
+    for i in range(NSTEP // 2):
+        gather(NSTEP // 2 + i)
+        pair_products(step_ref, change_ref, acc_ref, 2 * i)
+        pair_products(step_ref, change_ref, acc_ref, 2 * i + 1)
+    for i in range(NSTEP):
+        gather(NSTEP + i)
+        pair_products(step_ref, change_ref, acc_ref, count // 2 + i)
     for k in range(subs * NSTEP):
         rows_ref[0, k : k + 1, :] = seen_ref[k]
-    for copy in copies:
-        copy.wait()
-    pairs_kernel(step_ref, change_ref, gram_ref, acc_ref)
+    pair_sums(acc_ref, rows, gram_ref)
 
 
 def outer_kernel(
@@ -268,8 +295,8 @@
     state_ref[:, :, :, longs - longs % LANES :] = jnp.zeros((subs * NSTEP, levels, 8, LANES), F32)
     take_rows(rows_ref, cell_ref, lane_ref)
 
-    def tangent(j, _):
-        sub, lev = j // levels, j % levels
+    def tangent(sub, lev):
+        j = sub * levels + lev
         x, push = inc_ref[sub, lev, :8], forcing_ref[sub, lev, :8]
         lat, lon = lat_ref[lev, :8], lon_ref[lev, :8]
         rest = 1.0 - lat - lon
@@ -279,13 +306,11 @@
             x = rest * x + lat * above + lon * west(x) + push
             state_ref[sub * NSTEP + step, lev, :, :longs] = x
         end_ref[sub, lev] = x
-        return 0
-
-    lax.fori_loop(0, subs * levels, tangent, 0)
-    sent_ref[:, :8] = end_ref[subs - 1]
-    sent_ref[:, 8:] = upper_ref[subs - 1]
-
-    def gather(k, _):
+        if sub == subs - 1:
+            sent_ref[lev, :8] = x
+            sent_ref[lev, 8:] = upper_ref[sub, lev]
+
+    def gather(k):
         part = []
         for t in range(tiles):
             part += four_rows(state_ref, k, 0, t)
@@ -298,15 +323,11 @@
             seen_ref[k, :, part] = value
 
         look_up(blocks, INNER, cell_ref[k].astype(jnp.int16), lane_ref[k], store)
-        return 0
-
-    lax.fori_loop(0, subs * NSTEP, gather, 0, unroll=2)
 
     slot = lax.broadcasted_iota(jnp.int32, (NSTEP, slots), 1)
     row = lax.broadcasted_iota(jnp.int32, (NSTEP, slots), 0)
-    for copy in copies:
-        copy.wait()
-    for sub in range(subs):
+
+    def departures(sub):
         ks = range(sub * NSTEP, (sub + 1) * NSTEP)
         seen = rows_ref[0, ks.start : ks.stop, :]
         seen = seen + jnp.concatenate([seen_ref[k] for k in ks], axis=0)
@@ -318,29 +339,43 @@
         for step in range(NSTEP):
             dep_row[ks[step]] = dep[step : step + 1]
 
-    def scatter(k, _):
+    def scatter(k):
         cell = cell_ref[k].astype(jnp.int16)
         out = spread(one_hot(INNER, EDGE, cell), lane_ref[k], dep_row[k])
         store_four(inject_ref, k, 0, out, 0, tiles)
-        return 0
-
-    lax.fori_loop(0, subs * NSTEP, scatter, 0, unroll=2)
-
-    for sub in range(subs):
-        for lev in range(levels):
-            j = sub * levels + lev
-            later = next_ref[lev, :8] if sub == subs - 1 else inc_ref[sub + 1, lev, :8]
-            d = ew_ref[lev, :8] * (later - end_ref[sub, lev])
-            if sub == subs - 1:
-                d = d * last_ref[0]
-            lat, lon = lat_ref[lev, :8], lon_ref[lev, :8]
-            rest = 1.0 - lat - lon
-            for step in range(NSTEP - 1, -1, -1):
-                d = d + inject_ref[sub * NSTEP + step, lev]
-                part = lat * d
-                edge_ref[j, step : step + 1, :] = part[:1, :]
-                if step:
-                    d = rest * d + pltpu.roll(part, 7, 0) + east(lon * d)
+
+    def dual_edge(sub, lev):
+        j = sub * levels + lev
+        later = next_ref[lev, :8] if sub == subs - 1 else inc_ref[sub + 1, lev, :8]
+        d = ew_ref[lev, :8] * (later - end_ref[sub, lev])
+        if sub == subs - 1:
+            d = d * last_ref[0]
+        lat, lon = lat_ref[lev, :8], lon_ref[lev, :8]
+        rest = 1.0 - lat - lon
+        for step in range(NSTEP - 1, -1, -1):
+            d = d + inject_ref[sub * NSTEP + step, lev]
+            part = lat * d
+            edge_ref[j, step : step + 1, :] = part[:1, :]
+            if step:
+                d = rest * d + pltpu.roll(part, 7, 0) + east(lon * d)
+
+    for lev in range(levels):
+        tangent(0, lev)
+    for i in range(NSTEP):
+        gather(i)
+        tangent(1, i)
+    for copy in copies:
+        copy.wait()
+    departures(0)
+    for i in range(NSTEP):
+        gather(NSTEP + i)
+        scatter(i)
+    departures(1)
+    for i in range(NSTEP):
+        scatter(NSTEP + i)
+        dual_edge(0, i)
+    for lev in range(levels):
+        dual_edge(1, lev)
 
 
 def spread(hot, lane, dep):
@@ -396,7 +431,7 @@
         store_four(lower_ref, k, 4, out[high:], 0, tiles)
         return 0
 
-    lax.fori_loop(0, count, one, 0, unroll=2)
+    lax.fori_loop(0, count, one, 0, unroll=8)
 
 
 def gradient_kernel(
@@ -452,21 +487,16 @@
                 dots_ref[which * pairs + i] += fold(g * ref[i, sub, lev].astype(F32))
         return 0
 
-    lax.fori_loop(0, count, one, 0)
+    lax.fori_loop(0, count, one, 0, unroll=2)
     sums = [jnp.sum(dots_ref[v], axis=0, keepdims=True) for v in range(2 * pairs)]
     sums = jnp.concatenate(sums, axis=0)
     dots = jnp.sum(sums, axis=1, keepdims=True)
-    raw = gram_ref[...]
-    row = lax.broadcasted_iota(jnp.int32, raw.shape, 0)
-    col = lax.broadcasted_iota(jnp.int32, raw.shape, 1)
-    group = col // rows
-    here = col % rows == row
-    out = jnp.zeros((1, raw.shape[1]), F32)
-    for c in range(pairs):
-        part = jnp.sum(jnp.where(group == c, raw, 0.0), axis=1, keepdims=True)
-        out += jnp.sum(jnp.where(here & (group == c), part, 0.0), axis=0, keepdims=True)
-    stats_ref[0:1, :] = out
-    stats_ref[1:2, :] = jnp.sum(jnp.where(here, dots, 0.0), axis=0, keepdims=True)
+    row, group, inner = lane_places(gram_ref.shape)
+    ahead = (group - row) % pairs
+    moved = jnp.concatenate([dots[pairs:], dots[:pairs]], axis=0)
+    out = jnp.where(ahead == WITH_CHANGE, dots, jnp.where(ahead == WITH_STEP, moved, gram_ref[...]))
+    out = jnp.where(row < pairs, gram_ref[...], out)
+    stats_ref[...] = jnp.sum(jnp.where(inner == row, out, 0.0), axis=0, keepdims=True)
 
 
 def fold(x):
@@ -492,20 +522,24 @@
     count = subs * levels
     handed = pltpu.make_async_copy(grad_ref, grad_out, sems.at[count])
     handed.start()
-    gram = jnp.sum(stats_ref[:, 0, :], axis=0, keepdims=True)
-    dots = jnp.sum(stats_ref[:, 1, :], axis=0, keepdims=True)
+    stats = jnp.sum(stats_ref[...], axis=0, keepdims=True)
     shape = (both, LANES)
-    row = lax.broadcasted_iota(jnp.int32, shape, 0)
-    col = lax.broadcasted_iota(jnp.int32, shape, 1)
-    group, inner = col // both, col % both
-    gram = jnp.broadcast_to(gram, shape)
-    dots = jnp.broadcast_to(dots, shape)
+    row, group, inner = lane_places(shape)
+    gram = jnp.broadcast_to(stats, shape)
 
     def column(mask, x):
         return jnp.sum(jnp.where(mask, x, 0.0), axis=1, keepdims=True)
 
-    dots = column((inner == row) & (group == 0), dots)
-    by_change = [column((inner == row) & (group == c), gram) for c in range(pairs)]
+    order = row % pairs
+    changes = row >= pairs
+    ahead = jnp.where(changes, WITH_CHANGE, WITH_STEP)
+    dots = column((inner == pairs + order) & (group == (order + ahead) % pairs), gram)
+
+    def with_change_of(c):
+        swap = changes & ((c - order) % pairs >= WITH_CHANGE)
+        return (group == jnp.where(swap, order, c)) & (inner == jnp.where(swap, pairs + c, row))
+
+    by_change = [column(with_change_of(c), gram) for c in range(pairs)]
     by_step = [column((group == row) & (inner == i), gram)[:pairs] for i in range(pairs)]
     diagonal = column((group == row) & (inner == row), gram)[:pairs]
     rho = 1.0 / diagonal
@@ -542,7 +576,7 @@
         copy(j).start()
         return 0
 
-    lax.fori_loop(0, count, one, 0)
+    lax.fori_loop(0, count, one, 0, unroll=2)
     for j in range(count):
         copy(j).wait()
     handed.wait()
@@ -576,9 +610,6 @@
     def floats(*shape):
         return pltpu.VMEM(shape, F32)
 
-    def cost(flops):
-        return pl.CostEstimate(flops=flops, bytes_accessed=1 << 20, transcendentals=0)
-
     def far(*arrays):
         return [pltpu.with_memory_space_constraint(x, pltpu.HBM) for x in arrays]
 
@@ -589,7 +620,7 @@
         out_specs=[WHOLE] * (2 + len(arguments)),
         out_shape=[floats(levels, rows, longs), floats(count, NSTEP, longs)]
         + [like(x) for x in arguments],
-        scratch_shapes=[pltpu.SemaphoreType.DMA((len(arguments) + 1,))],
+        scratch_shapes=[pltpu.SemaphoreType.DMA((len(arguments) + 5,))],
         compiler_params=params(16),
         name="edge",
     )(*far(*arguments))
@@ -602,27 +633,24 @@
         pltpu.VMEM(row_shape, jnp.int32),
         pltpu.VMEM(row_shape, jnp.int32),
     ]
-    rows_of_slots, end_high, gram = pl.pallas_call(
+    rows_of_slots, end_high, gram, steps, changes = pl.pallas_call(
         inner_kernel,
         in_specs=[WHOLE] * 5 + [FAR] * 2,
-        out_specs=[WHOLE] * 3,
+        out_specs=[WHOLE] * 5,
         out_shape=[
             floats(3, subs * NSTEP, slots),
             floats(subs, levels, 8, longs),
             floats(2 * pairs, pairs * rows),
+            like(pair_step),
+            like(pair_change),
         ],
         scratch_shapes=[
             pltpu.VMEM((subs * NSTEP, levels, rows, wide), F32),
-            pltpu.VMEM((2 * pairs * rows, pairs * rows), F32),
+            pltpu.VMEM((pairs * rows, 2 * pairs * rows), F32),
         ]
         + row_scratch
-        + [
-            pltpu.VMEM(pair_step.shape, BF16),
-            pltpu.VMEM(pair_step.shape, BF16),
-            pltpu.SemaphoreType.DMA((2,)),
-        ],
+        + [pltpu.SemaphoreType.DMA((2, pairs))],
         compiler_params=params(28),
-        cost_estimate=cost(8 * 10**9),
         name="inner",
     )(inc, push, lat, lon, index, *far(pair_step, pair_change))
 
@@ -645,7 +673,6 @@
         + row_scratch
         + [pltpu.VMEM(row_shape, F32), pltpu.SemaphoreType.DMA((2,))],
         compiler_params=params(24),
-        cost_estimate=cost(5 * 10**9),
         name="outer",
     )(
         last,
@@ -661,8 +688,8 @@
         rows_of_slots,
         end_high,
     )
+    previous = shifted(sent, "tm", 1)
     below = shifted(edge, "space", -1)
-    previous = shifted(sent, "tm", 1)
 
     lower, upper = pl.pallas_call(
         scatter_kernel,
@@ -671,7 +698,7 @@
         out_shape=[floats(subs * NSTEP, levels, 8, longs)] * 2,
         scratch_shapes=row_scratch[1:] + row_scratch[:1],
         compiler_params=params(24),
-        cost_estimate=cost(6 * 10**9),
+        cost_estimate=pl.CostEstimate(flops=6 * 10**9, bytes_accessed=1 << 20, transcendentals=0),
         name="scatter",
     )(rows_of_slots, dep, part)
 
@@ -679,7 +706,7 @@
         gradient_kernel,
         in_specs=[SCALAR] + [WHOLE] * 14,
         out_specs=[WHOLE] * 2,
-        out_shape=[like(increment), floats(2, LANES)],
+        out_shape=[like(increment), floats(1, LANES)],
         scratch_shapes=[pltpu.VMEM((2 * pairs, 8, LANES), F32)],
         compiler_params=params(16),
         name="gradient",
@@ -697,12 +724,12 @@
         upper,
         below,
         gram,
-        pair_step,
-        pair_change,
+        steps,
+        changes,
     )
 
     stats = jnp.broadcast_to(stats[None], (devices,) + stats.shape)
-    stats = lax.all_to_all(stats, ("tm", "space"), 0, 0)
+    stats = lax.all_to_all(stats, ("tm", "space"), 0, 0).reshape(devices, LANES)
 
     return pl.pallas_call(
         direction_kernel,
@@ -716,7 +743,7 @@
         ],
         compiler_params=params(16),
         name="direction",
-    )(stats, gradient, pair_step, pair_change)
+    )(stats, gradient, steps, changes)
 
 
 def solution(mesh):

time: 74.1 us -> 63.3 us (0.85)
  Pallas kernels: 38.9 us -> 29.5 us
  local copies, waits for them, and re-layouts: 1.64 us -> 0.09 us
    pallas_call x1, Pallas kernels: 11.3 us -> 7.1 us  [on_device(): pl.pallas_call(outer_kernel, in_specs=[SCALAR] + [WHOLE] * 7 + [SCALAR] +...]
    pallas_call x1, Pallas kernels: 10.6 us -> 8.62 us  [on_device(): pl.pallas_call(inner_kernel, in_specs=[WHOLE] * 5 + [FAR] * 2, out_specs=...]
    pallas_call x1, Pallas kernels: 4.55 us -> 2.75 us  [on_device(): pl.pallas_call(edge_kernel, in_specs=[FAR] * len(arguments), out_specs=[W...]
    unnamed x10 -> x2, local copies, waits for them, and re-layouts: 1.61 us -> 0.01 us
where the time goes in v3:
time: 63.3 us; the launch traced here: 63.1 us
  Pallas kernels  29.5 us (47%)
  blocking collectives  20.8 us (33%)
  starting transfers between devices  11.8 us (19%)
  between operations  0.92 us (1%)
    all_to_all x1, blocking collectives, on_device(): stats = lax.all_to_all(stats, ('tm', 'space'), 0, 0).reshape(devices, LANES)  20.8 us
    ppermute x4, starting transfers between devices, shifted(): return lax.ppermute(shard, axis, pairs)  11.8 us
    pallas_call x1, Pallas kernels, on_device(): pl.pallas_call(inner_kernel, in_specs=[WHOLE] * 5 + [FAR] * 2, out_specs=...  8.62 us
    pallas_call x1, Pallas kernels, on_device(): pl.pallas_call(outer_kernel, in_specs=[SCALAR] + [WHOLE] * 7 + [SCALAR] +...  7.1 us
    pallas_call x1, Pallas kernels, on_device(): pl.pallas_call(scatter_kernel, in_specs=[WHOLE] * 3, out_specs=[WHOLE] *...  5.09 us
    pallas_call x1, Pallas kernels, on_device(): pl.pallas_call(gradient_kernel, in_specs=[SCALAR] + [WHOLE] * 14, out_spe...  3.39 us
    pallas_call x1, Pallas kernels, on_device(): pl.pallas_call(edge_kernel, in_specs=[FAR] * len(arguments), out_specs=[W...  2.75 us
    pallas_call x1, Pallas kernels, on_device(): pl.pallas_call(direction_kernel, in_specs=[WHOLE] * 4, out_specs=[FAR] *...  2.53 us
  transfers between devices with their start and end apart: 4, of which 0 were waited for; matrix products, arithmetic and copies ran while one was open for 0% of the time, Pallas kernels for 22%

profile of v3, /device:TPU:1, one launch (start us, length us, event | category | flops | bytes accessed | tf_op | source)
XLA Modules:
  0.0 63.1 jit_solution(13766172001711653473)
XLA Ops:
  0.6 2.8 %edge.1 = (f32[4,16,1440]{2,1,0:T(8,128)}, f32[8,4,1440]{2,1,0:T(4,128)}, f32[2,4,16,1440]{3,2,1,0:T(8,128)S(1)}, f32[2,4,16,1440]{3,2,1,0:T(8,128)S(1)}, f32[4,...) custom-call(f32[2,4,16,1440]{3,2,1,0:T(8,128)} %refs_0_.1, ...), custom_call_target="tpu_custom_call" | custom-call | tf_op jit(solution)/shard_map/edge/pallas_call | solution.py:617
  3.4 3.3 %collective-permute-start = (f32[4,16,1440]{2,1,0:T(8,128)}, f32[4,16,1440]{2,1,0:T(8,128)S(1)}, u32[]{:S(2)}, u32[]{:S(2)}) collective-permute-start(f32[4,16,1440]{2,1,0:T(8,128)} %get-tuple-element.28), channel_id=1, source_target_pairs={{16,0},{32,16},{48,32},{64,48},{80,64},{96,80},{112,96},{17,1},{33... | collective-permute-start | bytes 1105928 | tf_op jit(solution)/shard_map/ppermute | solution.py:22
  6.7 3.3 %collective-permute-start.1 = (f32[8,4,1440]{2,1,0:T(4,128)}, f32[8,4,1440]{2,1,0:T(4,128)S(1)}, u32[]{:S(2)}, u32[]{:S(2)}) collective-permute-start(f32[8,4,1440]{2,1,0:T(4,128)} %get-tuple-element.30), channel_id=1, source_target_pairs={{0,1},{1,2},{2,3},{3,4},{4,5},{5,6},{6,7},{7,8},{8,9},{9,10},{10,1... | collective-permute-start | bytes 552968 | tf_op jit(solution)/shard_map/ppermute | solution.py:22
  10.0 0.0 copy-start
  10.1 8.6 %inner.1 = (f32[3,8,2048]{2,1,0:T(8,128)S(1)}, f32[2,4,8,1440]{3,2,1,0:T(8,128)S(1)}, f32[16,128]{1,0:T(8,128)S(1)}, bf16[8,2,4,16,1440]{4,3,2,1,0:T(8,128)(2,1)S(1)}, bf16[8,2,4,16,1440]{4,3,2,1,0:T(8,128)(2,1)S(1)}) custom-call(f32[2,4,16,1440]{3,2,1,0:T(8,128)S(1)} %get-tuple-element.24.inc_ref, f32[2,4,16,1440]{3,2,1,0:T(8,128)S(1)} %get-tuple-element.29.forcing_ref, ...), custom_call_target="tpu_custom_call" | custom-call | tf_op jit(solution)/shard_map/inner/pallas_call | solution.py:636
  18.7 0.0 collective-permute-done.1.above_ref
  18.7 0.0 collective-permute-done.next_ref
  18.7 0.0 copy-done
  18.7 7.1 %outer.1 = (f32[2,4,8,1440]{3,2,1,0:T(8,128)S(1)}, f32[4,16,1440]{2,1,0:T(8,128)S(1)}, f32[8,4,1440]{2,1,0:T(4,128)S(1)}, f32[8,4,8,1440]{3,2,1,0:T(8,128)S(1)}, f32[8,2048]{1,0:T(8,128)S(1)}) custom-call(f32[1]{0:T(128)} %bitcast.last_ref, f32[2,4,16,1440]{3,2,1,0:T(8,128)S(1)} %get-tuple-element.24.inc_ref, ...), custom_call_target="tpu_custom_call" | custom-call | tf_op jit(solution)/shard_map/outer/pallas_call | solution.py:657
  25.8 1.5 %collective-permute-start.3 = (f32[8,4,1440]{2,1,0:T(4,128)S(1)}, f32[8,4,1440]{2,1,0:T(4,128)S(1)}, u32[]{:S(2)}, u32[]{:S(2)}) collective-permute-start(f32[8,4,1440]{2,1,0:T(4,128)S(1)} %get-tuple-element.40), channel_id=1, source_target_pairs={{1,0},{2,1},{3,2},{4,3},{5,4},{6,5},{7,6},{8,7},{9,8},{10,9},{11,1... | collective-permute-start | bytes 552968 | tf_op jit(solution)/shard_map/ppermute | solution.py:22
  27.3 3.7 %collective-permute-start.2 = (f32[4,16,1440]{2,1,0:T(8,128)S(1)}, f32[4,16,1440]{2,1,0:T(8,128)S(1)}, u32[]{:S(2)}, u32[]{:S(2)}) collective-permute-start(f32[4,16,1440]{2,1,0:T(8,128)S(1)} %get-tuple-element.35), channel_id=1, source_target_pairs={{0,16},{16,32},{32,48},{48,64},{64,80},{80,96},{96,112},{1,17},{17... | collective-permute-start | bytes 1105928 | tf_op jit(solution)/shard_map/ppermute | solution.py:22
  31.0 5.1 %scatter.1 = (f32[8,4,8,1440]{3,2,1,0:T(8,128)S(1)}, f32[8,4,8,1440]{3,2,1,0:T(8,128)S(1)}) custom-call(f32[3,8,2048]{2,1,0:T(8,128)S(1)} %get-tuple-element.32.rows_ref, f32[8,2048]{1,0:T(8,128)S(1)} %get-tuple-element.36.dep_ref, f32[8,4,8,1440]{3,2,1,0:T(8,128)S(1)} %get-tuple-element.37.part_ref), custom_call_target="tpu_custom_call" | custom-call | flops 6000000000 | bytes 1048576 | tf_op jit(solution)/shard_map/scatter/pallas_call | solution.py:694
  36.1 0.0 collective-permute-done.3.below_ref
  36.1 0.0 collective-permute-done.2.previous_ref
  36.2 3.4 %gradient.1 = (f32[2,4,16,1440]{3,2,1,0:T(8,128)S(1)}, f32[1,128]{1,0:T(1,128)S(1)}) custom-call(f32[1]{0:T(128)} %bitcast.last_ref, f32[2,4,16,1440]{3,2,1,0:T(8,128)S(1)} %get-tuple-element.24.inc_ref, f32[4,16,1440]{2,1,0:T(8,128)S(1)} %get-tuple-element.25.lat_ref, f32[4,16,1440]{2,1,0:T(8,128)S(1)} %get-tuple-element.26.lon_ref, ...), custom_call_target="tpu_custom_call" | custom-call | tf_op jit(solution)/shard_map/gradient/pallas_call | solution.py:705
  39.5 0.1 broadcast_in_dim.9
  39.6 20.8 %all_to_all.5 = f32[128,1,128]{2,1,0:T(1,128)S(1)} all-to-all(f32[128,1,128]{2,1,0:T(1,128)S(1)} %broadcast_in_dim.9), channel_id=1, replica_groups=mesh['tm'=8,'space'=16] {'tm','space'}, dimensions={0} | all-to-all | bytes 131072 | tf_op jit(solution)/shard_map/all_to_all | solution.py:732
  60.4 2.5 %direction.1 = (f32[2,4,16,1440]{3,2,1,0:T(8,128)}, f32[2,4,16,1440]{3,2,1,0:T(8,128)}) custom-call(f32[128,128]{1,0:T(8,128)S(1)} %bitcast.4, f32[2,4,16,1440]{3,2,1,0:T(8,128)S(1)} %get-tuple-element.45.grad_ref, bf16[8,2,4,16,1440]{4,3,2,1,0:T(8,128)(2,1)S(1)} %get-tuple-element.42.step_ref, bf16[8,2,4,16,1440]{4,3,2,1,0:T(8,128)(2,1)S(1)} %get-tuple-element.43.change_ref), custom_call_target="tpu_custom_call" | custom-call | tf_op jit(solution)/shard_map/direction/pallas_call | solution.py:734
Async XLA Ops:
  3.4 15.3 %collective-permute-start = (f32[4,16,1440]{2,1,0:T(8,128)}, f32[4,16,1440]{2,1,0:T(8,128)S(1)}, u32[]{:S(2)}, u32[]{:S(2)}) collective-permute-start(f32[4,16,1440]{2,1,0:T(8,128)} %get-tuple-element.28), channel_id=1, source_target_pairs={{16,0},{32,16},{48,32},{64,48},{80,64},{96,80},{112,96},{17,1},{33... | collective-permute-start | bytes 1105928 | tf_op jit(solution)/shard_map/ppermute | solution.py:22
  6.7 12.0 %collective-permute-start.1 = (f32[8,4,1440]{2,1,0:T(4,128)}, f32[8,4,1440]{2,1,0:T(4,128)S(1)}, u32[]{:S(2)}, u32[]{:S(2)}) collective-permute-start(f32[8,4,1440]{2,1,0:T(4,128)} %get-tuple-element.30), channel_id=1, source_target_pairs={{0,1},{1,2},{2,3},{3,4},{4,5},{5,6},{6,7},{7,8},{8,9},{9,10},{10,1... | collective-permute-start | bytes 552968 | tf_op jit(solution)/shard_map/ppermute | solution.py:22
  10.0 8.7 %copy-start = (s32[2,4,1]{1,2,0:T(1,128)S(1)}, s32[2,4,1]{1,2,0:T(1,128)}, u32[]{:S(2)}) copy-start(s32[2,4,1]{1,2,0:T(1,128)} %param.17) | copy-start | bytes 100
  25.8 10.3 %collective-permute-start.3 = (f32[8,4,1440]{2,1,0:T(4,128)S(1)}, f32[8,4,1440]{2,1,0:T(4,128)S(1)}, u32[]{:S(2)}, u32[]{:S(2)}) collective-permute-start(f32[8,4,1440]{2,1,0:T(4,128)S(1)} %get-tuple-element.40), channel_id=1, source_target_pairs={{1,0},{2,1},{3,2},{4,3},{5,4},{6,5},{7,6},{8,7},{9,8},{10,9},{11,1... | collective-permute-start | bytes 552968 | tf_op jit(solution)/shard_map/ppermute | solution.py:22
  27.3 8.8 %collective-permute-start.2 = (f32[4,16,1440]{2,1,0:T(8,128)S(1)}, f32[4,16,1440]{2,1,0:T(8,128)S(1)}, u32[]{:S(2)}, u32[]{:S(2)}) collective-permute-start(f32[4,16,1440]{2,1,0:T(8,128)S(1)} %get-tuple-element.35), channel_id=1, source_target_pairs={{0,16},{16,32},{32,48},{48,64},{64,80},{80,96},{96,112},{1,17},{17... | collective-permute-start | bytes 1105928 | tf_op jit(solution)/shard_map/ppermute | solution.py:22

commit v4 on v3

--- a/solution.py
+++ b/solution.py
@@ -44,7 +44,7 @@
 
 
 def edge_kernel(*refs):
-    sources, (following_ref, edge_ref), homes, sems = refs[:6], refs[6:8], refs[8:14], refs[14]
+    sources, (following_ref, edge_ref), homes, sems = refs[:5], refs[5:7], refs[7:12], refs[12]
     def lower(ref):
         return ref.at[:, :, 8:] if len(ref.shape) == 4 else ref.at[:, 8:]
 
@@ -155,11 +155,13 @@
     index_ref,
     step_far,
     change_far,
+    ew_far,
     rows_ref,
     end_ref,
     gram_ref,
     step_ref,
     change_ref,
+    ew_ref,
     state_ref,
     acc_ref,
     seen_ref,
@@ -173,6 +175,7 @@
         for i in range(step_ref.shape[0])
         for which, (far, near) in enumerate(((step_far, step_ref), (change_far, change_ref)))
     ]
+    copies.append(pltpu.make_async_copy(ew_far, ew_ref, sems.at[2, 0]))
     for copy in copies:
         copy.start()
     tiles = -(-longs // LANES)
@@ -241,7 +244,7 @@
         gather(i)
         tangent(1, 2 * i)
         tangent(1, 2 * i + 1)
-    for copy in copies:
+    for copy in copies[:-1]:
         copy.wait()
     for i in range(NSTEP // 2):
         gather(NSTEP // 2 + i)
@@ -253,6 +256,7 @@
     for k in range(subs * NSTEP):
         rows_ref[0, k : k + 1, :] = seen_ref[k]
     pair_sums(acc_ref, rows, gram_ref)
+    copies[-1].wait()
 
 
 def outer_kernel(
@@ -434,38 +438,35 @@
     lax.fori_loop(0, count, one, 0, unroll=8)
 
 
-def gradient_kernel(
+def add_gradient(
+    sub,
     last_ref,
     inc_ref,
     lat_ref,
     lon_ref,
     ew_ref,
-    next_ref,
+    later_ref,
+    earlier_ref,
     end_low_ref,
     end_high_ref,
-    previous_ref,
     lower_ref,
     upper_ref,
     below_ref,
-    gram_ref,
     step_ref,
     change_ref,
     grad_ref,
-    stats_ref,
     dots_ref,
 ):
     subs, levels, rows, longs = inc_ref.shape
     pairs = step_ref.shape[0]
-    count = subs * levels
-    dots_ref[...] = jnp.zeros_like(dots_ref)
-
-    def one(j, _):
-        sub, lev = j // levels, j % levels
+
+    def one(lev, _):
         ew = ew_ref[lev]
-        final = sub == subs - 1
-        later = jnp.where(final, next_ref[lev], inc_ref[jnp.minimum(sub + 1, subs - 1), lev])
-        d = ew * (later - jnp.concatenate([end_low_ref[sub, lev], end_high_ref[sub, lev]], axis=0))
-        d = d * jnp.where(final, last_ref[0], 1.0)
+        end = jnp.concatenate([end_low_ref[sub, lev], end_high_ref[sub, lev]], axis=0)
+        if sub == subs - 1:
+            d = ew * (later_ref[lev] - end) * last_ref[0]
+        else:
+            d = ew * (inc_ref[sub + 1, lev] - end)
         lat, lon = lat_ref[lev], lon_ref[lev]
         rest = 1.0 - lat - lon
         bottom = rows_of(d) == rows - 1
@@ -473,21 +474,49 @@
             k = sub * NSTEP + step
             d = d + jnp.concatenate([lower_ref[k, lev], upper_ref[k, lev]], axis=0)
             part = lat * d
-            below = jnp.where(
-                bottom, below_ref[j, step : step + 1, :], pltpu.roll(part, rows - 1, 0)
+            below = below_ref[sub * levels + lev, step : step + 1, :]
+            below = jnp.where(bottom, below, pltpu.roll(part, rows - 1, 0))
+            d = rest * d + below + east(lon * d)
+        if sub == 0:
+            earlier = earlier_ref[lev]
+        else:
+            earlier = jnp.concatenate(
+                [end_low_ref[sub - 1, lev], end_high_ref[sub - 1, lev]], axis=0
             )
-            d = rest * d + below + east(lon * d)
-        before = jnp.maximum(sub - 1, 0)
-        before = jnp.concatenate([end_low_ref[before, lev], end_high_ref[before, lev]], axis=0)
-        earlier = jnp.where(sub == 0, previous_ref[lev], before)
         g = ew * (inc_ref[sub, lev] - earlier) - d
-        grad_ref[sub, lev] = g
+        grad_ref[lev] = g
         for i in range(pairs):
             for which, ref in enumerate((step_ref, change_ref)):
                 dots_ref[which * pairs + i] += fold(g * ref[i, sub, lev].astype(F32))
         return 0
 
-    lax.fori_loop(0, count, one, 0, unroll=2)
+    lax.fori_loop(0, levels, one, 0, unroll=2)
+
+
+def second_kernel(last_ref, inc_ref, lat_ref, lon_ref, ew_ref, next_ref, *refs):
+    dots_ref = refs[-1]
+    dots_ref[...] = jnp.zeros_like(dots_ref)
+    sub = inc_ref.shape[0] - 1
+    add_gradient(sub, last_ref, inc_ref, lat_ref, lon_ref, ew_ref, next_ref, None, *refs)
+
+
+def first_kernel(inc_ref, lat_ref, lon_ref, ew_ref, previous_ref, *refs):
+    dots_in, gram_ref, grad_ref, stats_ref, dots_ref = refs[-5:]
+    pairs = gram_ref.shape[0] // 2
+    dots_ref[...] = dots_in[...]
+    add_gradient(
+        0,
+        None,
+        inc_ref,
+        lat_ref,
+        lon_ref,
+        ew_ref,
+        None,
+        previous_ref,
+        *refs[:-5],
+        grad_ref,
+        dots_ref,
+    )
     sums = [jnp.sum(dots_ref[v], axis=0, keepdims=True) for v in range(2 * pairs)]
     sums = jnp.concatenate(sums, axis=0)
     dots = jnp.sum(sums, axis=1, keepdims=True)
@@ -515,13 +544,19 @@
 
 
 def direction_kernel(
-    stats_ref, grad_ref, step_ref, change_ref, grad_out, direction_out, coef_ref, out_ref, sems
+    stats_ref, first_ref, second_ref, step_ref, change_ref, grad_out, direction_out, coef_ref,
+    out_ref, sems,
 ):
     pairs, subs, levels, _, _ = step_ref.shape
     both = 2 * pairs
     count = subs * levels
-    handed = pltpu.make_async_copy(grad_ref, grad_out, sems.at[count])
-    handed.start()
+    grads = (first_ref, second_ref)
+    handed = [
+        pltpu.make_async_copy(ref, grad_out.at[sub], sems.at[count + sub])
+        for sub, ref in enumerate(grads)
+    ]
+    for copy in handed:
+        copy.start()
     stats = jnp.sum(stats_ref[...], axis=0, keepdims=True)
     shape = (both, LANES)
     row, group, inner = lane_places(shape)
@@ -560,26 +595,22 @@
         coef_ref[pairs + i] = jnp.broadcast_to(-gamma * alphas[i], (8, LANES))
 
 
-    def copy(j):
-        sub, lev = j // levels, j % levels
-        return pltpu.make_async_copy(
-            out_ref.at[sub, lev], direction_out.at[sub, lev], sems.at[j]
-        )
-
-    def one(j, _):
-        sub, lev = j // levels, j % levels
-        total = coef_ref[both][:1, :1] * grad_ref[sub, lev]
-        for i in range(pairs):
-            total += coef_ref[i][:1, :1] * step_ref[i, sub, lev].astype(F32)
-            total += coef_ref[pairs + i][:1, :1] * change_ref[i, sub, lev].astype(F32)
-        out_ref[sub, lev] = total
-        copy(j).start()
-        return 0
-
-    lax.fori_loop(0, count, one, 0, unroll=2)
-    for j in range(count):
-        copy(j).wait()
-    handed.wait()
+    copies = []
+    for sub in range(subs):
+        for lev in range(levels):
+            total = coef_ref[both][:1, :1] * grads[sub][lev]
+            for i in range(pairs):
+                total += coef_ref[i][:1, :1] * step_ref[i, sub, lev].astype(F32)
+                total += coef_ref[pairs + i][:1, :1] * change_ref[i, sub, lev].astype(F32)
+            out_ref[sub, lev] = total
+            copies.append(
+                pltpu.make_async_copy(
+                    out_ref.at[sub, lev], direction_out.at[sub, lev], sems.at[len(copies)]
+                )
+            )
+            copies[-1].start()
+    for copy in copies + handed:
+        copy.wait()
 
 
 def on_device(
@@ -613,8 +644,8 @@
     def far(*arrays):
         return [pltpu.with_memory_space_constraint(x, pltpu.HBM) for x in arrays]
 
-    arguments = (increment, forcing, lat_courant, lon_courant, error_weight, site_index)
-    following, edge, inc, push, lat, lon, ew, index = pl.pallas_call(
+    arguments = (increment, forcing, lat_courant, lon_courant, site_index)
+    following, edge, inc, push, lat, lon, index = pl.pallas_call(
         edge_kernel,
         in_specs=[FAR] * len(arguments),
         out_specs=[WHOLE] * (2 + len(arguments)),
@@ -633,26 +664,27 @@
         pltpu.VMEM(row_shape, jnp.int32),
         pltpu.VMEM(row_shape, jnp.int32),
     ]
-    rows_of_slots, end_high, gram, steps, changes = pl.pallas_call(
+    rows_of_slots, end_high, gram, steps, changes, ew = pl.pallas_call(
         inner_kernel,
-        in_specs=[WHOLE] * 5 + [FAR] * 2,
-        out_specs=[WHOLE] * 5,
+        in_specs=[WHOLE] * 5 + [FAR] * 3,
+        out_specs=[WHOLE] * 6,
         out_shape=[
             floats(3, subs * NSTEP, slots),
             floats(subs, levels, 8, longs),
             floats(2 * pairs, pairs * rows),
             like(pair_step),
             like(pair_change),
+            like(error_weight),
         ],
         scratch_shapes=[
             pltpu.VMEM((subs * NSTEP, levels, rows, wide), F32),
             pltpu.VMEM((pairs * rows, 2 * pairs * rows), F32),
         ]
         + row_scratch
-        + [pltpu.SemaphoreType.DMA((2, pairs))],
+        + [pltpu.SemaphoreType.DMA((3, pairs))],
         compiler_params=params(28),
         name="inner",
-    )(inc, push, lat, lon, index, *far(pair_step, pair_change))
+    )(inc, push, lat, lon, index, *far(pair_step, pair_change, error_weight))
 
     end_low, sent, edge, part, dep = pl.pallas_call(
         outer_kernel,
@@ -702,48 +734,41 @@
         name="scatter",
     )(rows_of_slots, dep, part)
 
-    gradient, stats = pl.pallas_call(
-        gradient_kernel,
-        in_specs=[SCALAR] + [WHOLE] * 14,
+    shared = (end_low, end_high, lower, upper, below, steps, changes)
+    grad_second, dots = pl.pallas_call(
+        second_kernel,
+        in_specs=[SCALAR] + [WHOLE] * 12,
         out_specs=[WHOLE] * 2,
-        out_shape=[like(increment), floats(1, LANES)],
+        out_shape=[floats(levels, rows, longs), floats(2 * pairs, 8, LANES)],
+        compiler_params=params(16),
+        name="second",
+    )(last, inc, lat, lon, ew, following, *shared)
+    grad_first, stats = pl.pallas_call(
+        first_kernel,
+        in_specs=[WHOLE] * 14,
+        out_specs=[WHOLE] * 2,
+        out_shape=[floats(levels, rows, longs), floats(1, LANES)],
         scratch_shapes=[pltpu.VMEM((2 * pairs, 8, LANES), F32)],
         compiler_params=params(16),
-        name="gradient",
-    )(
-        last,
-        inc,
-        lat,
-        lon,
-        ew,
-        following,
-        end_low,
-        end_high,
-        previous,
-        lower,
-        upper,
-        below,
-        gram,
-        steps,
-        changes,
-    )
+        name="first",
+    )(inc, lat, lon, ew, previous, *shared, dots, gram)
 
     stats = jnp.broadcast_to(stats[None], (devices,) + stats.shape)
     stats = lax.all_to_all(stats, ("tm", "space"), 0, 0).reshape(devices, LANES)
 
     return pl.pallas_call(
         direction_kernel,
-        in_specs=[WHOLE] * 4,
+        in_specs=[WHOLE] * 5,
         out_specs=[FAR] * 2,
         out_shape=[jax.ShapeDtypeStruct(increment.shape, F32)] * 2,
         scratch_shapes=[
             pltpu.VMEM((2 * pairs + 1, 8, LANES), F32),
             pltpu.VMEM(increment.shape, F32),
-            pltpu.SemaphoreType.DMA((count + 1,)),
+            pltpu.SemaphoreType.DMA((count + subs,)),
         ],
         compiler_params=params(16),
         name="direction",
-    )(stats, gradient, steps, changes)
+    )(stats, grad_first, grad_second, steps, changes)
 
 
 def solution(mesh):

time: 63.3 us -> 62.2 us (0.983)
  blocking collectives: 20.8 us -> 20.1 us
    all_to_all x1, blocking collectives: 20.8 us -> 20.1 us  [on_device(): stats = lax.all_to_all(stats, ('tm', 'space'), 0, 0).reshape(devices, LANES)]
    pallas_call x3 -> x4, Pallas kernels: 14.5 us -> 14.3 us  [the longest x1 8.71 us: on_device(): pl.pallas_call(inner_kernel, in_specs=[WHOLE] * 5 + [FAR] * 3, out_specs=...]
  transfers between devices with their start and end apart: 4 -> 4, of which waited for: 0 -> 0; matrix products, arithmetic and copies ran while one was open for 0% -> 0% of each run, Pallas kernels for 22% -> 25%
where the time goes in v4:
time: 62.2 us; the launch traced here: 62 us
  Pallas kernels  29.1 us (47%)
  blocking collectives  20.1 us (32%)
  starting transfers between devices  11.8 us (19%)
  between operations  0.93 us (1%)
    all_to_all x1, blocking collectives, on_device(): stats = lax.all_to_all(stats, ('tm', 'space'), 0, 0).reshape(devices, LANES)  20.1 us
    ppermute x4, starting transfers between devices, shifted(): return lax.ppermute(shard, axis, pairs)  11.8 us
    pallas_call x1, Pallas kernels, on_device(): pl.pallas_call(inner_kernel, in_specs=[WHOLE] * 5 + [FAR] * 3, out_specs=...  8.71 us
    pallas_call x1, Pallas kernels, on_device(): pl.pallas_call(outer_kernel, in_specs=[SCALAR] + [WHOLE] * 7 + [SCALAR] +...  7.12 us
    pallas_call x1, Pallas kernels, on_device(): pl.pallas_call(scatter_kernel, in_specs=[WHOLE] * 3, out_specs=[WHOLE] *...  5.1 us
    pallas_call x1, Pallas kernels, on_device(): pl.pallas_call(edge_kernel, in_specs=[FAR] * len(arguments), out_specs=[W...  2.61 us
    pallas_call x1, Pallas kernels, on_device(): pl.pallas_call(direction_kernel, in_specs=[WHOLE] * 5, out_specs=[FAR] *...  2.17 us
    pallas_call x1, Pallas kernels, on_device(): pl.pallas_call(first_kernel, in_specs=[WHOLE] * 14, out_specs=[WHOLE] * 2...  1.75 us
  transfers between devices with their start and end apart: 4, of which 0 were waited for; matrix products, arithmetic and copies ran while one was open for 0% of the time, Pallas kernels for 25%

profile of v4, /device:TPU:1, one launch (start us, length us, event | category | flops | bytes accessed | tf_op | source)
XLA Modules:
  0.0 62.0 jit_solution(11982201498220493927)
XLA Ops:
  0.6 2.6 %edge.1 = (f32[4,16,1440]{2,1,0:T(8,128)S(1)}, f32[8,4,1440]{2,1,0:T(4,128)}, f32[2,4,16,1440]{3,2,1,0:T(8,128)S(1)}, f32[2,4,16,1440]{3,2,1,0:T(8,128)S(1)}, f3...) custom-call(f32[2,4,16,1440]{3,2,1,0:T(8,128)} %refs_0_.1, ...), custom_call_target="tpu_custom_call" | custom-call | tf_op jit(solution)/shard_map/edge/pallas_call | solution.py:648
  3.2 3.3 %collective-permute-start = (f32[4,16,1440]{2,1,0:T(8,128)S(1)}, f32[4,16,1440]{2,1,0:T(8,128)S(1)}, u32[]{:S(2)}, u32[]{:S(2)}) collective-permute-start(f32[4,16,1440]{2,1,0:T(8,128)S(1)} %get-tuple-element.32), channel_id=1, source_target_pairs={{16,0},{32,16},{48,32},{64,48},{80,64},{96,80},{112,96},{17,1},{33... | collective-permute-start | bytes 1105928 | tf_op jit(solution)/shard_map/ppermute | solution.py:22
  6.6 3.3 %collective-permute-start.1 = (f32[8,4,1440]{2,1,0:T(4,128)}, f32[8,4,1440]{2,1,0:T(4,128)S(1)}, u32[]{:S(2)}, u32[]{:S(2)}) collective-permute-start(f32[8,4,1440]{2,1,0:T(4,128)} %get-tuple-element.33), channel_id=1, source_target_pairs={{0,1},{1,2},{2,3},{3,4},{4,5},{5,6},{6,7},{7,8},{8,9},{9,10},{10,1... | collective-permute-start | bytes 552968 | tf_op jit(solution)/shard_map/ppermute | solution.py:22
  9.9 0.0 copy-start
  9.9 8.7 %inner.1 = (f32[3,8,2048]{2,1,0:T(8,128)S(1)}, f32[2,4,8,1440]{3,2,1,0:T(8,128)S(1)}, f32[16,128]{1,0:T(8,128)S(1)}, bf16[8,2,4,16,1440]{4,3,2,1,0:T(8,128)(2,1)...) custom-call(f32[2,4,16,1440]{3,2,1,0:T(8,128)S(1)} %get-tuple-element.26.inc_ref, ...), custom_call_target="tpu_custom_call" | custom-call | tf_op jit(solution)/shard_map/inner/pallas_call | solution.py:667
  18.6 0.0 collective-permute-done.1.above_ref
  18.6 0.0 collective-permute-done.next_ref
  18.6 0.0 copy-done
  18.7 7.1 %outer.1 = (f32[2,4,8,1440]{3,2,1,0:T(8,128)S(1)}, f32[4,16,1440]{2,1,0:T(8,128)S(1)}, f32[8,4,1440]{2,1,0:T(4,128)S(1)}, f32[8,4,8,1440]{3,2,1,0:T(8,128)S(1)}, f32[8,2048]{1,0:T(8,128)S(1)}) custom-call(f32[1]{0:T(128)} %bitcast.last_ref, f32[2,4,16,1440]{3,2,1,0:T(8,128)S(1)} %get-tuple-element.26.inc_ref, ...), custom_call_target="tpu_custom_call" | custom-call | tf_op jit(solution)/shard_map/outer/pallas_call | solution.py:689
  25.8 1.5 %collective-permute-start.3 = (f32[8,4,1440]{2,1,0:T(4,128)S(1)}, f32[8,4,1440]{2,1,0:T(4,128)S(1)}, u32[]{:S(2)}, u32[]{:S(2)}) collective-permute-start(f32[8,4,1440]{2,1,0:T(4,128)S(1)} %get-tuple-element.42), channel_id=1, source_target_pairs={{1,0},{2,1},{3,2},{4,3},{5,4},{6,5},{7,6},{8,7},{9,8},{10,9},{11,1... | collective-permute-start | bytes 552968 | tf_op jit(solution)/shard_map/ppermute | solution.py:22
  27.3 3.7 %collective-permute-start.2 = (f32[4,16,1440]{2,1,0:T(8,128)S(1)}, f32[4,16,1440]{2,1,0:T(8,128)S(1)}, u32[]{:S(2)}, u32[]{:S(2)}) collective-permute-start(f32[4,16,1440]{2,1,0:T(8,128)S(1)} %get-tuple-element.36), channel_id=1, source_target_pairs={{0,16},{16,32},{32,48},{48,64},{64,80},{80,96},{96,112},{1,17},{17... | collective-permute-start | bytes 1105928 | tf_op jit(solution)/shard_map/ppermute | solution.py:22
  31.0 5.1 %scatter.1 = (f32[8,4,8,1440]{3,2,1,0:T(8,128)S(1)}, f32[8,4,8,1440]{3,2,1,0:T(8,128)S(1)}) custom-call(f32[3,8,2048]{2,1,0:T(8,128)S(1)} %get-tuple-element.34.rows_ref, f32[8,2048]{1,0:T(8,128)S(1)} %get-tuple-element.38.dep_ref, f32[8,4,8,1440]{3,2,1,0:T(8,128)S(1)} %get-tuple-element.39.part_ref), custom_call_target="tpu_custom_call" | custom-call | flops 6000000000 | bytes 1048576 | tf_op jit(solution)/shard_map/scatter/pallas_call | solution.py:726
  36.1 0.0 collective-permute-done.3.refs_4_
  36.1 1.6 %second.1 = (f32[4,16,1440]{2,1,0:T(8,128)S(1)}, f32[16,8,128]{2,1,0:T(8,128)S(1)}) custom-call(f32[1]{0:T(128)} %bitcast.last_ref, f32[2,4,16,1440]{3,2,1,0:T(8,128)S(1)} %get-tuple-element.26.inc_ref, f32[4,16,1440]{2,1,0:T(8,128)S(1)} %get-tuple-element.27.lat_ref, f32[4,16,1440]{2,1,0:T(8,128)S(1)} %get-tuple-element.28.lon_ref, ...), custom_call_target="tpu_custom_call" | custom-call | tf_op jit(solution)/shard_map/second/pallas_call | solution.py:738
  37.7 0.0 collective-permute-done.2.previous_ref
  37.8 1.7 %first.1 = (f32[4,16,1440]{2,1,0:T(8,128)S(1)}, f32[1,128]{1,0:T(1,128)S(1)}) custom-call(f32[2,4,16,1440]{3,2,1,0:T(8,128)S(1)} %get-tuple-element.26.inc_ref, f32[4,16,1440]{2,1,0:T(8,128)S(1)} %get-tuple-element.27.lat_ref, f32[4,16,1440]{2,1,0:T(8,128)S(1)} %get-tuple-element.28.lon_ref, f32[4,16,1440]{2,1,0:T(8,128)S(1)} %get-tuple-element.31.ew_ref, ...), custom_call_target="tpu_custom_call" | custom-call | tf_op jit(solution)/shard_map/first/pallas_call | solution.py:746
  39.5 0.1 broadcast_in_dim.9
  39.6 20.1 %all_to_all.5 = f32[128,1,128]{2,1,0:T(1,128)S(1)} all-to-all(f32[128,1,128]{2,1,0:T(1,128)S(1)} %broadcast_in_dim.9), channel_id=1, replica_groups=mesh['tm'=8,'space'=16] {'tm','space'}, dimensions={0} | all-to-all | bytes 131072 | tf_op jit(solution)/shard_map/all_to_all | solution.py:757
  59.7 2.2 %direction.1 = (f32[2,4,16,1440]{3,2,1,0:T(8,128)}, f32[2,4,16,1440]{3,2,1,0:T(8,128)}) custom-call(f32[128,128]{1,0:T(8,128)S(1)} %bitcast.4, f32[4,16,1440]{2,1,0:T(8,128)S(1)} %get-tuple-element.48.first_ref, f32[4,16,1440]{2,1,0:T(8,128)S(1)} %get-tuple-element.49.second_ref, bf16[8,2,4,16,1440]{4,3,2,1,0:T(8,128)(2,1)S(1)} %get-tuple-element.43.refs_5_.step_ref, ...), custom_call_target="tpu_custom_call" | custom-call | tf_op jit(solution)/shard_map/direction/pallas_call | solution.py:759
Async XLA Ops:
  3.2 15.4 %collective-permute-start = (f32[4,16,1440]{2,1,0:T(8,128)S(1)}, f32[4,16,1440]{2,1,0:T(8,128)S(1)}, u32[]{:S(2)}, u32[]{:S(2)}) collective-permute-start(f32[4,16,1440]{2,1,0:T(8,128)S(1)} %get-tuple-element.32), channel_id=1, source_target_pairs={{16,0},{32,16},{48,32},{64,48},{80,64},{96,80},{112,96},{17,1},{33... | collective-permute-start | bytes 1105928 | tf_op jit(solution)/shard_map/ppermute | solution.py:22
  6.6 12.0 %collective-permute-start.1 = (f32[8,4,1440]{2,1,0:T(4,128)}, f32[8,4,1440]{2,1,0:T(4,128)S(1)}, u32[]{:S(2)}, u32[]{:S(2)}) collective-permute-start(f32[8,4,1440]{2,1,0:T(4,128)} %get-tuple-element.33), channel_id=1, source_target_pairs={{0,1},{1,2},{2,3},{3,4},{4,5},{5,6},{6,7},{7,8},{8,9},{9,10},{10,1... | collective-permute-start | bytes 552968 | tf_op jit(solution)/shard_map/ppermute | solution.py:22
  9.9 8.8 %copy-start = (s32[2,4,1]{1,2,0:T(1,128)S(1)}, s32[2,4,1]{1,2,0:T(1,128)}, u32[]{:S(2)}) copy-start(s32[2,4,1]{1,2,0:T(1,128)} %param.17) | copy-start | bytes 100
  25.8 10.3 %collective-permute-start.3 = (f32[8,4,1440]{2,1,0:T(4,128)S(1)}, f32[8,4,1440]{2,1,0:T(4,128)S(1)}, u32[]{:S(2)}, u32[]{:S(2)}) collective-permute-start(f32[8,4,1440]{2,1,0:T(4,128)S(1)} %get-tuple-element.42), channel_id=1, source_target_pairs={{1,0},{2,1},{3,2},{4,3},{5,4},{6,5},{7,6},{8,7},{9,8},{10,9},{11,1... | collective-permute-start | bytes 552968 | tf_op jit(solution)/shard_map/ppermute | solution.py:22
  27.3 10.5 %collective-permute-start.2 = (f32[4,16,1440]{2,1,0:T(8,128)S(1)}, f32[4,16,1440]{2,1,0:T(8,128)S(1)}, u32[]{:S(2)}, u32[]{:S(2)}) collective-permute-start(f32[4,16,1440]{2,1,0:T(8,128)S(1)} %get-tuple-element.36), channel_id=1, source_target_pairs={{0,16},{16,32},{32,48},{48,64},{64,80},{80,96},{96,112},{1,17},{17... | collective-permute-start | bytes 1105928 | tf_op jit(solution)/shard_map/ppermute | solution.py:22

commit v5 on v4

--- a/solution.py
+++ b/solution.py
@@ -158,12 +158,10 @@
     ew_far,
     rows_ref,
     end_ref,
-    gram_ref,
     step_ref,
     change_ref,
     ew_ref,
     state_ref,
-    acc_ref,
     seen_ref,
     cell_ref,
     lane_ref,
@@ -237,26 +235,18 @@
         return 0
 
     lax.fori_loop(0, levels, first, 0, unroll=2)
-    acc_ref[...] = jnp.zeros_like(acc_ref)
-
-    count = subs * levels
     for i in range(NSTEP // 2):
         gather(i)
         tangent(1, 2 * i)
         tangent(1, 2 * i + 1)
-    for copy in copies[:-1]:
-        copy.wait()
     for i in range(NSTEP // 2):
         gather(NSTEP // 2 + i)
-        pair_products(step_ref, change_ref, acc_ref, 2 * i)
-        pair_products(step_ref, change_ref, acc_ref, 2 * i + 1)
     for i in range(NSTEP):
         gather(NSTEP + i)
-        pair_products(step_ref, change_ref, acc_ref, count // 2 + i)
     for k in range(subs * NSTEP):
         rows_ref[0, k : k + 1, :] = seen_ref[k]
-    pair_sums(acc_ref, rows, gram_ref)
-    copies[-1].wait()
+    for copy in copies:
+        copy.wait()
 
 
 def outer_kernel(
@@ -456,11 +446,14 @@
     change_ref,
     grad_ref,
     dots_ref,
+    beside=None,
 ):
     subs, levels, rows, longs = inc_ref.shape
     pairs = step_ref.shape[0]
 
     def one(lev, _):
+        if beside is not None:
+            beside(lev)
         ew = ew_ref[lev]
         end = jnp.concatenate([end_low_ref[sub, lev], end_high_ref[sub, lev]], axis=0)
         if sub == subs - 1:
@@ -494,16 +487,40 @@
 
 
 def second_kernel(last_ref, inc_ref, lat_ref, lon_ref, ew_ref, next_ref, *refs):
-    dots_ref = refs[-1]
+    step_ref, change_ref, grad_ref, dots_ref, acc_ref = refs[-5:]
+    subs, levels, _, _ = inc_ref.shape
     dots_ref[...] = jnp.zeros_like(dots_ref)
-    sub = inc_ref.shape[0] - 1
-    add_gradient(sub, last_ref, inc_ref, lat_ref, lon_ref, ew_ref, next_ref, None, *refs)
+    acc_ref[...] = jnp.zeros_like(acc_ref)
+
+    def beside(lev):
+        pair_products(step_ref, change_ref, acc_ref, (subs - 1) * levels + lev)
+
+    add_gradient(
+        subs - 1,
+        last_ref,
+        inc_ref,
+        lat_ref,
+        lon_ref,
+        ew_ref,
+        next_ref,
+        None,
+        *refs[:-3],
+        grad_ref,
+        dots_ref,
+        beside,
+    )
 
 
 def first_kernel(inc_ref, lat_ref, lon_ref, ew_ref, previous_ref, *refs):
-    dots_in, gram_ref, grad_ref, stats_ref, dots_ref = refs[-5:]
-    pairs = gram_ref.shape[0] // 2
+    dots_in, products_ref, grad_ref, stats_ref, dots_ref, acc_ref, gram_ref = refs[-7:]
+    step_ref, change_ref = refs[-9:-7]
+    pairs, _, _, rows, _ = step_ref.shape
     dots_ref[...] = dots_in[...]
+    acc_ref[...] = products_ref[...]
+
+    def beside(lev):
+        pair_products(step_ref, change_ref, acc_ref, lev)
+
     add_gradient(
         0,
         None,
@@ -513,10 +530,12 @@
         ew_ref,
         None,
         previous_ref,
-        *refs[:-5],
+        *refs[:-7],
         grad_ref,
         dots_ref,
+        beside,
     )
+    pair_sums(acc_ref, rows, gram_ref)
     sums = [jnp.sum(dots_ref[v], axis=0, keepdims=True) for v in range(2 * pairs)]
     sums = jnp.concatenate(sums, axis=0)
     dots = jnp.sum(sums, axis=1, keepdims=True)
@@ -664,21 +683,19 @@
         pltpu.VMEM(row_shape, jnp.int32),
         pltpu.VMEM(row_shape, jnp.int32),
     ]
-    rows_of_slots, end_high, gram, steps, changes, ew = pl.pallas_call(
+    rows_of_slots, end_high, steps, changes, ew = pl.pallas_call(
         inner_kernel,
         in_specs=[WHOLE] * 5 + [FAR] * 3,
-        out_specs=[WHOLE] * 6,
+        out_specs=[WHOLE] * 5,
         out_shape=[
             floats(3, subs * NSTEP, slots),
             floats(subs, levels, 8, longs),
-            floats(2 * pairs, pairs * rows),
             like(pair_step),
             like(pair_change),
             like(error_weight),
         ],
         scratch_shapes=[
             pltpu.VMEM((subs * NSTEP, levels, rows, wide), F32),
-            pltpu.VMEM((pairs * rows, 2 * pairs * rows), F32),
         ]
         + row_scratch
         + [pltpu.SemaphoreType.DMA((3, pairs))],
@@ -735,11 +752,15 @@
     )(rows_of_slots, dep, part)
 
     shared = (end_low, end_high, lower, upper, below, steps, changes)
-    grad_second, dots = pl.pallas_call(
+    grad_second, dots, products = pl.pallas_call(
         second_kernel,
         in_specs=[SCALAR] + [WHOLE] * 12,
-        out_specs=[WHOLE] * 2,
-        out_shape=[floats(levels, rows, longs), floats(2 * pairs, 8, LANES)],
+        out_specs=[WHOLE] * 3,
+        out_shape=[
+            floats(levels, rows, longs),
+            floats(2 * pairs, 8, LANES),
+            floats(pairs * rows, 2 * pairs * rows),
+        ],
         compiler_params=params(16),
         name="second",
     )(last, inc, lat, lon, ew, following, *shared)
@@ -748,10 +769,14 @@
         in_specs=[WHOLE] * 14,
         out_specs=[WHOLE] * 2,
         out_shape=[floats(levels, rows, longs), floats(1, LANES)],
-        scratch_shapes=[pltpu.VMEM((2 * pairs, 8, LANES), F32)],
+        scratch_shapes=[
+            pltpu.VMEM((2 * pairs, 8, LANES), F32),
+            pltpu.VMEM(products.shape, F32),
+            pltpu.VMEM((2 * pairs, pairs * rows), F32),
+        ],
         compiler_params=params(16),
         name="first",
-    )(inc, lat, lon, ew, previous, *shared, dots, gram)
+    )(inc, lat, lon, ew, previous, *shared, dots, products)
 
     stats = jnp.broadcast_to(stats[None], (devices,) + stats.shape)
     stats = lax.all_to_all(stats, ("tm", "space"), 0, 0).reshape(devices, LANES)

time: 62.2 us -> 60.9 us (0.979)
  Pallas kernels: 29.1 us -> 27.8 us
    pallas_call x1, Pallas kernels: 8.71 us -> 6.67 us  [on_device(): pl.pallas_call(inner_kernel, in_specs=[WHOLE] * 5 + [FAR] * 3, out_specs=...]
  transfers between devices with their start and end apart: 4 -> 4, of which waited for: 0 -> 0; matrix products, arithmetic and copies ran while one was open for 0% -> 0% of each run, Pallas kernels for 25% -> 23%
where the time goes in v5:
time: 60.9 us; the launch traced here: 60.7 us
  Pallas kernels  27.8 us (46%)
  blocking collectives  20.1 us (33%)
  starting transfers between devices  11.8 us (19%)
  between operations  0.93 us (2%)
    all_to_all x1, blocking collectives, on_device(): stats = lax.all_to_all(stats, ('tm', 'space'), 0, 0).reshape(devices, LANES)  20.1 us
    ppermute x4, starting transfers between devices, shifted(): return lax.ppermute(shard, axis, pairs)  11.8 us
    pallas_call x1, Pallas kernels, on_device(): pl.pallas_call(outer_kernel, in_specs=[SCALAR] + [WHOLE] * 7 + [SCALAR] +...  7.1 us
    pallas_call x1, Pallas kernels, on_device(): pl.pallas_call(inner_kernel, in_specs=[WHOLE] * 5 + [FAR] * 3, out_specs=...  6.67 us
    pallas_call x1, Pallas kernels, on_device(): pl.pallas_call(scatter_kernel, in_specs=[WHOLE] * 3, out_specs=[WHOLE] *...  5.1 us
    pallas_call x1, Pallas kernels, on_device(): pl.pallas_call(edge_kernel, in_specs=[FAR] * len(arguments), out_specs=[W...  2.61 us
    pallas_call x1, Pallas kernels, on_device(): pl.pallas_call(first_kernel, in_specs=[WHOLE] * 14, out_specs=[WHOLE] * 2...  2.19 us
    pallas_call x1, Pallas kernels, on_device(): pl.pallas_call(direction_kernel, in_specs=[WHOLE] * 5, out_specs=[FAR] *...  2.17 us
  transfers between devices with their start and end apart: 4, of which 0 were waited for; matrix products, arithmetic and copies ran while one was open for 0% of the time, Pallas kernels for 23%

profile of v5, /device:TPU:1, one launch (start us, length us, event | category | flops | bytes accessed | tf_op | source)
XLA Modules:
  0.0 60.7 jit_solution(13713218018671887260)
XLA Ops:
  0.6 2.6 %edge.1 = (f32[4,16,1440]{2,1,0:T(8,128)S(1)}, f32[8,4,1440]{2,1,0:T(4,128)}, f32[2,4,16,1440]{3,2,1,0:T(8,128)S(1)}, f32[2,4,16,1440]{3,2,1,0:T(8,128)S(1)}, f3...) custom-call(f32[2,4,16,1440]{3,2,1,0:T(8,128)} %refs_0_.1, ...), custom_call_target="tpu_custom_call" | custom-call | tf_op jit(solution)/shard_map/edge/pallas_call | solution.py:667
  3.2 3.3 %collective-permute-start = (f32[4,16,1440]{2,1,0:T(8,128)S(1)}, f32[4,16,1440]{2,1,0:T(8,128)S(1)}, u32[]{:S(2)}, u32[]{:S(2)}) collective-permute-start(f32[4,16,1440]{2,1,0:T(8,128)S(1)} %get-tuple-element.32), channel_id=1, source_target_pairs={{16,0},{32,16},{48,32},{64,48},{80,64},{96,80},{112,96},{17,1},{33... | collective-permute-start | bytes 1105928 | tf_op jit(solution)/shard_map/ppermute | solution.py:22
  6.6 3.3 %collective-permute-start.1 = (f32[8,4,1440]{2,1,0:T(4,128)}, f32[8,4,1440]{2,1,0:T(4,128)S(1)}, u32[]{:S(2)}, u32[]{:S(2)}) collective-permute-start(f32[8,4,1440]{2,1,0:T(4,128)} %get-tuple-element.33), channel_id=1, source_target_pairs={{0,1},{1,2},{2,3},{3,4},{4,5},{5,6},{6,7},{7,8},{8,9},{9,10},{10,1... | collective-permute-start | bytes 552968 | tf_op jit(solution)/shard_map/ppermute | solution.py:22
  9.9 0.0 copy-start
  9.9 6.7 %inner.1 = (f32[3,8,2048]{2,1,0:T(8,128)S(1)}, f32[2,4,8,1440]{3,2,1,0:T(8,128)S(1)}, bf16[8,2,4,16,1440]{4,3,2,1,0:T(8,128)(2,1)S(1)}, bf16[8,2,4,16,1440]{4,3,2,1,0:T(8,128)(2,1)S(1)}, f32[4,16,1440]{2,1,0:T(8,128)S(1)}) custom-call(f32[2,4,16,1440]{3,2,1,0:T(8,128)S(1)} %get-tuple-element.26.inc_ref, ...), custom_call_target="tpu_custom_call" | custom-call | tf_op jit(solution)/shard_map/inner/pallas_call | solution.py:686
  16.6 0.0 collective-permute-done.1.above_ref
  16.6 0.0 collective-permute-done.next_ref
  16.6 0.0 copy-done
  16.6 7.1 %outer.1 = (f32[2,4,8,1440]{3,2,1,0:T(8,128)S(1)}, f32[4,16,1440]{2,1,0:T(8,128)S(1)}, f32[8,4,1440]{2,1,0:T(4,128)S(1)}, f32[8,4,8,1440]{3,2,1,0:T(8,128)S(1)}, f32[8,2048]{1,0:T(8,128)S(1)}) custom-call(f32[1]{0:T(128)} %bitcast.last_ref, f32[2,4,16,1440]{3,2,1,0:T(8,128)S(1)} %get-tuple-element.26.inc_ref, ...), custom_call_target="tpu_custom_call" | custom-call | tf_op jit(solution)/shard_map/outer/pallas_call | solution.py:706
  23.7 1.3 %collective-permute-start.3 = (f32[8,4,1440]{2,1,0:T(4,128)S(1)}, f32[8,4,1440]{2,1,0:T(4,128)S(1)}, u32[]{:S(2)}, u32[]{:S(2)}) collective-permute-start(f32[8,4,1440]{2,1,0:T(4,128)S(1)} %get-tuple-element.42), channel_id=1, source_target_pairs={{1,0},{2,1},{3,2},{4,3},{5,4},{6,5},{7,6},{8,7},{9,8},{10,9},{11,1... | collective-permute-start | bytes 552968 | tf_op jit(solution)/shard_map/ppermute | solution.py:22
  25.0 3.9 %collective-permute-start.2 = (f32[4,16,1440]{2,1,0:T(8,128)S(1)}, f32[4,16,1440]{2,1,0:T(8,128)S(1)}, u32[]{:S(2)}, u32[]{:S(2)}) collective-permute-start(f32[4,16,1440]{2,1,0:T(8,128)S(1)} %get-tuple-element.36), channel_id=1, source_target_pairs={{0,16},{16,32},{32,48},{48,64},{64,80},{80,96},{96,112},{1,17},{17... | collective-permute-start | bytes 1105928 | tf_op jit(solution)/shard_map/ppermute | solution.py:22
  28.9 5.1 %scatter.1 = (f32[8,4,8,1440]{3,2,1,0:T(8,128)S(1)}, f32[8,4,8,1440]{3,2,1,0:T(8,128)S(1)}) custom-call(f32[3,8,2048]{2,1,0:T(8,128)S(1)} %get-tuple-element.34.rows_ref, f32[8,2048]{1,0:T(8,128)S(1)} %get-tuple-element.38.dep_ref, f32[8,4,8,1440]{3,2,1,0:T(8,128)S(1)} %get-tuple-element.39.part_ref), custom_call_target="tpu_custom_call" | custom-call | flops 6000000000 | bytes 1048576 | tf_op jit(solution)/shard_map/scatter/pallas_call | solution.py:743
  34.0 0.0 collective-permute-done.3.refs_4_
  34.0 2.0 %second.1 = (f32[4,16,1440]{2,1,0:T(8,128)S(1)}, f32[16,8,128]{2,1,0:T(8,128)S(1)}, f32[128,256]{1,0:T(8,128)S(1)}) custom-call(f32[1]{0:T(128)} %bitcast.last_ref, f32[2,4,16,1440]{3,2,1,0:T(8,128)S(1)} %get-tuple-element.26.inc_ref, f32[4,16,1440]{2,1,0:T(8,128)S(1)} %get-tuple-element.27.lat_ref, f32[4,16,1440]{2,1,0:T(8,128)S(1)} %get-tuple-element.28.lon_ref, ...), custom_call_target="tpu_custom_call" | custom-call | tf_op jit(solution)/shard_map/second/pallas_call | solution.py:755
  36.0 0.0 collective-permute-done.2.previous_ref
  36.0 2.2 %first.1 = (f32[4,16,1440]{2,1,0:T(8,128)S(1)}, f32[1,128]{1,0:T(1,128)S(1)}) custom-call(f32[2,4,16,1440]{3,2,1,0:T(8,128)S(1)} %get-tuple-element.26.inc_ref, f32[4,16,1440]{2,1,0:T(8,128)S(1)} %get-tuple-element.27.lat_ref, f32[4,16,1440]{2,1,0:T(8,128)S(1)} %get-tuple-element.28.lon_ref, f32[4,16,1440]{2,1,0:T(8,128)S(1)} %get-tuple-element.31.ew_ref, ...), custom_call_target="tpu_custom_call" | custom-call | tf_op jit(solution)/shard_map/first/pallas_call | solution.py:767
  38.2 20.1 %all_to_all.5 = f32[128,1,128]{2,1,0:T(1,128)S(1)} all-to-all(f32[128,1,128]{2,1,0:T(1,128)S(1)} %broadcast_in_dim.9), channel_id=1, replica_groups=mesh['tm'=8,'space'=16] {'tm','space'}, dimensions={0} | all-to-all | bytes 131072 | tf_op jit(solution)/shard_map/all_to_all | solution.py:782
  58.3 2.2 %direction.1 = (f32[2,4,16,1440]{3,2,1,0:T(8,128)}, f32[2,4,16,1440]{3,2,1,0:T(8,128)}) custom-call(f32[128,128]{1,0:T(8,128)S(1)} %bitcast.4, f32[4,16,1440]{2,1,0:T(8,128)S(1)} %get-tuple-element.48.first_ref, f32[4,16,1440]{2,1,0:T(8,128)S(1)} %get-tuple-element.49.second_ref, bf16[8,2,4,16,1440]{4,3,2,1,0:T(8,128)(2,1)S(1)} %get-tuple-element.43.refs_5_.step_ref, ...), custom_call_target="tpu_custom_call" | custom-call | tf_op jit(solution)/shard_map/direction/pallas_call | solution.py:784
  (1 shorter events, 0.0 us)
Async XLA Ops:
  3.2 13.3 %collective-permute-start = (f32[4,16,1440]{2,1,0:T(8,128)S(1)}, f32[4,16,1440]{2,1,0:T(8,128)S(1)}, u32[]{:S(2)}, u32[]{:S(2)}) collective-permute-start(f32[4,16,1440]{2,1,0:T(8,128)S(1)} %get-tuple-element.32), channel_id=1, source_target_pairs={{16,0},{32,16},{48,32},{64,48},{80,64},{96,80},{112,96},{17,1},{33... | collective-permute-start | bytes 1105928 | tf_op jit(solution)/shard_map/ppermute | solution.py:22
  6.6 10.0 %collective-permute-start.1 = (f32[8,4,1440]{2,1,0:T(4,128)}, f32[8,4,1440]{2,1,0:T(4,128)S(1)}, u32[]{:S(2)}, u32[]{:S(2)}) collective-permute-start(f32[8,4,1440]{2,1,0:T(4,128)} %get-tuple-element.33), channel_id=1, source_target_pairs={{0,1},{1,2},{2,3},{3,4},{4,5},{5,6},{6,7},{7,8},{8,9},{9,10},{10,1... | collective-permute-start | bytes 552968 | tf_op jit(solution)/shard_map/ppermute | solution.py:22
  9.9 6.7 %copy-start = (s32[2,4,1]{1,2,0:T(1,128)S(1)}, s32[2,4,1]{1,2,0:T(1,128)}, u32[]{:S(2)}) copy-start(s32[2,4,1]{1,2,0:T(1,128)} %param.17) | copy-start | bytes 100
  23.7 10.3 %collective-permute-start.3 = (f32[8,4,1440]{2,1,0:T(4,128)S(1)}, f32[8,4,1440]{2,1,0:T(4,128)S(1)}, u32[]{:S(2)}, u32[]{:S(2)}) collective-permute-start(f32[8,4,1440]{2,1,0:T(4,128)S(1)} %get-tuple-element.42), channel_id=1, source_target_pairs={{1,0},{2,1},{3,2},{4,3},{5,4},{6,5},{7,6},{8,7},{9,8},{10,9},{11,1... | collective-permute-start | bytes 552968 | tf_op jit(solution)/shard_map/ppermute | solution.py:22
  25.0 11.0 %collective-permute-start.2 = (f32[4,16,1440]{2,1,0:T(8,128)S(1)}, f32[4,16,1440]{2,1,0:T(8,128)S(1)}, u32[]{:S(2)}, u32[]{:S(2)}) collective-permute-start(f32[4,16,1440]{2,1,0:T(8,128)S(1)} %get-tuple-element.36), channel_id=1, source_target_pairs={{0,16},{16,32},{32,48},{48,64},{64,80},{80,96},{96,112},{1,17},{17... | collective-permute-start | bytes 1105928 | tf_op jit(solution)/shard_map/ppermute | solution.py:22
